TPU v7x, 256 devices: a whole 4x4x8 slice. The times are simulated.
256 devices in a mesh: row: 8 (over z), col: 16 (over y_lo, x, core), head: 2 (over y_hi).
Axes of the slice: x: 4, y: 4 (y_hi: 2, y_lo: 2; y = y_hi * 2 + y_lo), z: 8, core: 2. Of those that a mesh axis runs over, the one named last changes fastest.
Arguments:
- pair_field: bfloat16 [1024, 1024, 128], P('row', 'col'), may hold values from -6 to 6
- ln_gain: float32 [128], replicated, may hold values from 0.25 to 1.75
- w_query: bfloat16 [128, 128], P(None, 'head'), may hold values from -1 to 1
- w_key: bfloat16 [128, 128], P(None, 'head'), may hold values from -1 to 1
- w_value: bfloat16 [128, 128], P(None, 'head'), may hold values from -0.5 to 0.5
- w_gate: bfloat16 [128, 128], P(None, 'head'), may hold values from -0.5 to 0.5
- w_bias: bfloat16 [128, 4], P(None, 'head'), may hold values from -0.5 to 0.5
- w_out: bfloat16 [128, 128], replicated, may hold values from -3 to 3
- tile_mask: int32 [16, 16], replicated, may hold values from 0 to 1, as said below
- type_ids: int32 [1024], replicated, may hold values from 0 to 31, as said below
Outputs:
- pair_update: bfloat16 [1024, 1024, 128], P('row', 'col', 'head')
Inputs may be any that keep to these rules, and one draw needn't show every extreme that they name: `tile_mask`: 1 lets a block of 64 query tokens attend to a block of 64 key tokens; diagonal blocks are attended regardless. `type_ids`: 0 marks padding, which is never a key; the first of every 64 tokens is never padding.
All inputs are finite; a program needn't handle non-finite values.
Results may differ from a plain program's by a relative error of at most 0.012.
Values may be sent and summed in bfloat16 or wider, within the bound.
A program may use at most 128 MiB of HBM per device.

v0:
```python
import math

import jax
import jax.numpy as jnp
from jax import lax
from jax.sharding import PartitionSpec as P

epsilon = 1e-05
masked_score = -1000000000.0
start_best = -1e30


def partner_2(value, axis, stride):
    mask = 2**stride
    pairs = [(source, source ^ mask) for source in range(lax.axis_size(axis))]
    return lax.ppermute(value, axis, pairs)


def layer_norm(field, gain):
    wide = field.astype(jnp.float32)
    centred = wide - jnp.mean(wide, axis=-1, keepdims=True)
    spread = jnp.mean(centred * centred, axis=-1, keepdims=True)
    return (centred * lax.rsqrt(spread + epsilon) * gain).astype(jnp.bfloat16)


def project(normed, weight, heads):
    mapped = jnp.einsum("abc,cd->abd", normed, weight, preferred_element_type=jnp.float32)
    return mapped.reshape(mapped.shape[0], mapped.shape[1], heads, weight.shape[1] // heads)


def allowed_block(tile_mask, type_ids, query_start, query_count, key_count):
    blocks_count = tile_mask.shape[0]
    block_size = type_ids.shape[0] // blocks_count
    query_ids = query_start + jnp.arange(query_count, dtype=jnp.int32)
    key_ids = jnp.arange(key_count, dtype=jnp.int32)
    labels = jnp.arange(blocks_count, dtype=jnp.int32)
    query_blocks = query_ids // block_size
    key_blocks = key_ids // block_size
    pick_query = (query_blocks[:, None] == labels[None, :]).astype(jnp.float32)
    pick_key = (key_blocks[:, None] == labels[None, :]).astype(jnp.float32)
    contact = jnp.dot(jnp.dot(pick_query, tile_mask.astype(jnp.float32)), pick_key.T) > 0.5
    diagonal = query_blocks[:, None] == key_blocks[None, :]
    living = type_ids != 0
    return (contact | diagonal) & living[None, :]


def visit_keys(carried, query, keys, values, bias_part, allowed):
    scale = 1.0 / math.sqrt(query.shape[-1])
    running_max, running_sum, numerator = carried
    scores = (
        jnp.einsum("qjhd,kjhd->jhqk", query, keys, preferred_element_type=jnp.float32) * scale
        + bias_part[None]
    )
    scores = jnp.where(allowed[None, None], scores, masked_score)
    fresh_max = jnp.maximum(running_max, jnp.max(scores, axis=-1))
    exponent = jnp.exp(scores - fresh_max[..., None])
    running_sum = jnp.sum(exponent, axis=-1)
    numerator = jnp.einsum(
        "jhqk,kjhd->jhqd", exponent.astype(jnp.bfloat16), values, preferred_element_type=jnp.float32
    )
    return (fresh_max, running_sum, numerator)


def start_state(columns, heads, rows, depth):
    return (
        jnp.full((columns, heads, rows), start_best, jnp.float32),
        jnp.zeros((columns, heads, rows), jnp.float32),
        jnp.zeros((columns, heads, rows, depth), jnp.float32),
    )


def finish(carried, gate):
    running_max, running_sum, numerator = carried
    attention = jnp.transpose(numerator / running_sum[..., None], (2, 0, 1, 3))
    return (jax.nn.sigmoid(gate) * attention).astype(jnp.bfloat16)


def per_device(
    pair_field, ln_gain, w_query, w_key, w_value, w_gate, w_bias, w_out, tile_mask, type_ids
):
    row_count = lax.axis_size("row")
    col_count = lax.axis_size("col")
    tile_rows = pair_field.shape[0]
    tile_cols = pair_field.shape[1]
    total_rows = tile_rows * row_count
    heads = w_bias.shape[1]
    depth = w_query.shape[1] // heads
    block_count = tile_mask.shape[0]
    block_size = total_rows // block_count
    normed = layer_norm(pair_field, ln_gain)
    bias_tile = jnp.einsum(
        "abc,ch->abh", normed, w_bias, preferred_element_type=jnp.float32
    ).astype(jnp.bfloat16)
    strip = lax.all_to_all(normed, "row", split_axis=1, concat_axis=0, tiled=True)
    width = strip.shape[1]
    query = project(strip, w_query, heads).astype(jnp.bfloat16)
    keys = project(strip, w_key, heads).astype(jnp.bfloat16)
    values = project(strip, w_value, heads).astype(jnp.bfloat16)
    gate = project(strip, w_gate, heads)
    gathered = lax.all_gather(bias_tile[None], ("row", "col"), axis=0, tiled=True)
    gathered = gathered.reshape(row_count, col_count, tile_rows, tile_cols, heads)
    bias_full = jnp.transpose(gathered, (0, 2, 1, 3, 4)).reshape(total_rows, total_rows, heads)

    def query_block(block_index):
        start = block_index * block_size
        query_part = lax.dynamic_slice_in_dim(query, start, block_size, 0)
        gate_part = lax.dynamic_slice_in_dim(gate, start, block_size, 0)
        bias_part = jnp.transpose(
            lax.dynamic_slice_in_dim(bias_full, start, block_size, 1).astype(jnp.float32), (2, 1, 0)
        )
        initial = start_state(width, heads, block_size, depth)
        final = visit_keys(
            initial,
            query_part,
            keys,
            values,
            bias_part,
            allowed_block(tile_mask, type_ids, start, block_size, total_rows),
        )
        return finish(final, gate_part)

    blocks_out = lax.map(query_block, jnp.arange(block_count, dtype=jnp.int32))
    gated_strip = blocks_out.reshape(total_rows, width, heads * depth)
    gated = lax.all_to_all(gated_strip, "row", split_axis=0, concat_axis=1, tiled=True)
    head_index = lax.axis_index("head")
    half = w_out.shape[1] // 2
    span = heads * depth
    partner = partner_2(gated, "head", 0)
    own_cols = lax.dynamic_slice_in_dim(w_out, head_index * half, half, 1)
    own_rows = lax.dynamic_slice_in_dim(own_cols, head_index * span, span, 0)
    other_rows = lax.dynamic_slice_in_dim(own_cols, (1 - head_index) * span, span, 0)
    mixed = jnp.einsum(
        "abk,kc->abc", gated, own_rows, preferred_element_type=jnp.float32
    ) + jnp.einsum("abk,kc->abc", partner, other_rows, preferred_element_type=jnp.float32)
    return mixed.astype(jnp.bfloat16)


def solution(mesh):
    return jax.shard_map(
        per_device,
        mesh=mesh,
        in_specs=(
            P("row", "col", None),
            P(),
            P(None, "head"),
            P(None, "head"),
            P(None, "head"),
            P(None, "head"),
            P(None, "head"),
            P(),
            P(),
            P(),
        ),
        out_specs=P("row", "col", "head"),
        check_vma=False,
    )
```

profile of v0, /device:TPU:1, one launch (start us, length us, event | category | flops | bytes accessed | tf_op | source)
XLA Modules:
  0.0 480.1 jit_solution(7039563759008041328)
XLA Ops:
  6.5 3.5 convert_reduce_fusion
  10.1 6.1 %fusion.41 = f32[128,64]{0,1:T(8,128)S(1)} fusion(f32[128,64]{0,1:T(8,128)S(1)} %broadcast_multiply_fusion, bf16[128,64,128]{2,1,0:T(8,128)(2,1)S(1)} %copy-done.1), kind=kLoop, calls=%fused_computation.44 | loop fusion | flops 4186112 | bytes 2162688 | tf_op jit(solution)/shard_map/reduce_sum | solution.py:22
  16.2 4.9 %fusion.43 = bf16[128,64,128]{2,0,1:T(8,128)(2,1)S(1)} fusion(f32[128]{0:T(128)S(1)} %copy-done.10, f32[128,64]{0,1:T(8,128)S(1)} %add_rsqrt_fusion, f32[128,64]{0,1:T(8,128)S(1)} %broadcast_multiply_fusion, bf16[128,64,128]{2,1,0:T(8,128)(2,1)S(1)} %copy-done.1), kind=kLoop, calls=%fused_computation.46 | loop fusion | flops 5242880 | bytes 4260352 | tf_op jit(solution)/shard_map/convert_element_type | solution.py:23
  23.8 9.0 %all-to-all-start = ((bf16[128,64,128]{2,0,1:T(8,128)(2,1)}), bf16[128,64,128]{2,0,1:T(8,128)(2,1)S(1)}, u32[]{:S(2)}, u32[]{:S(2)}) async-start(bf16[128,64,128]{2,0,1:T(8,128)(2,1)} %copy-done.2), calls=%async_computation | async-start | bytes 4194304 | tf_op jit(solution)/shard_map/all_to_all | solution.py:94
  32.8 53.6 %all-to-all-done = bf16[128,64,128]{2,0,1:T(8,128)(2,1)S(1)} async-done(((bf16[128,64,128]{2,0,1:T(8,128)(2,1)}), bf16[128,64,128]{2,0,1:T(8,128)(2,1)S(1)}, u32[]{:S(2)}, u32[]{:S(2)}) %all-to-all-start) | async-done | bytes 2097184 | tf_op jit(solution)/shard_map/all_to_all | solution.py:94
  87.1 1.8 convolution_convert_fusion
  90.7 2.2 fusion.50
  92.9 163.5 %all-gather.3.cloned.1.call-done = bf16[16384,64,2]{0,1,2:T(8,128)(2,1)} async-done(((bf16[128,64,2]{0,1,2:T(8,128)(2,1)}), bf16[16384,64,2]{0,1,2:T(8,128)(2,1)}) %all-gather.3.cloned.1.call-update) | async-done | bytes 4194320 | tf_op jit(solution)/shard_map/all_gather | solution.py:100
  256.4 3.4 copy.48
  259.8 3.1 copy.36
  262.9 7.3 %reshape.89 = bf16[1024,1024,2]{0,1,2:T(8,128)(2,1)} reshape(bf16[8,128,16,64,2]{1,0,3,2,4:T(8,128)(2,1)} %copy.36) | data formatting | bytes 8388608 | tf_op jit(solution)/shard_map/reshape | solution.py:102
  270.2 132.9 %while.13 = (s32[]{:T(128)}, bf16[16,64,8,2,32]{1,4,3,2,0:T(8,128)(2,1)}, s32[16]{0:T(128)S(1)}, f32[1024,8,2,32]{0,3,2,1:T(8,128)}, bf16[16,16]{1,0:T(8,128)(2,...) while((s32[]{:T(128)}, ...), condition=%wide.region_5.6_spmd, body=%wide.region_2.5_spmd.sunk | while | flops 151644160 | bytes 22064876 | solution.py:122
  275.6 2.9 fusion.82
  281.2 1.4 fusion.80
  283.9 2.9 fusion.82
  292.2 2.9 fusion.82
  300.5 2.9 fusion.82
  306.1 1.4 fusion.80
  308.8 2.9 fusion.82
  317.1 2.9 fusion.82
  322.7 1.4 fusion.80
  325.4 2.9 fusion.82
  331.0 1.4 fusion.80
  333.7 2.9 fusion.82
  339.3 1.4 fusion.80
  342.0 2.9 fusion.82
  347.6 1.4 fusion.80
  350.3 2.9 fusion.82
  355.9 1.4 fusion.80
  358.6 2.9 fusion.82
  364.2 1.4 fusion.80
  366.9 2.9 fusion.82
  372.5 1.4 fusion.80
  375.2 2.9 fusion.82
  383.5 2.9 fusion.82
  389.1 1.4 fusion.80
  391.8 2.9 fusion.82
  397.4 1.4 fusion.80
  400.1 2.9 fusion.82
  403.0 3.0 copy.37
  406.0 1.5 reshape.90
  407.5 1.7 copy.38
  409.2 1.7 reshape.101
  410.9 32.9 %all_to_all.36 = bf16[8,2,32768]{2,1,0:T(2,128)(2,1)S(1)} all-to-all(bf16[8,2,32768]{2,1,0:T(2,128)(2,1)S(1)} %reshape.101), channel_id=1, replica_groups=mesh['row'=8,'col'=16,'head'=2] {'row'}, dimensions={0} | all-to-all | bytes 2097152 | tf_op jit(solution)/shard_map/all_to_all | solution.py:124
  443.8 1.4 reshape.102
  446.4 3.1 collective-permute-start
  450.1 21.6 %collective-permute-done = bf16[128,64,64]{0,2,1:T(8,128)(2,1)S(1)} collective-permute-done((bf16[128,64,64]{0,2,1:T(8,128)(2,1)S(1)}, bf16[128,64,64]{0,2,1:T(8,128)(2,1)S(1)}, u32[]{:S(2)}, u32[]{:S(2)}) %collective-permute-start) | collective-permute-done | bytes 1048608 | tf_op jit(solution)/shard_map/ppermute | solution.py:16
  471.7 1.5 add_convert_fusion
  (201 shorter events, 66.9 us)
Async XLA Ops:
  6.5 443.0 %copy-start = (bf16[128,128]{1,0:T(8,128)(2,1)S(1)}, bf16[128,128]{1,0:T(8,128)(2,1)}, u32[]{:S(2)}) copy-start(bf16[128,128]{1,0:T(8,128)(2,1)} %param.19) | copy-start | bytes 98308
  6.5 3.5 copy-start.1
  6.5 9.7 %copy-start.10 = (f32[128]{0:T(128)S(1)}, f32[128]{0:T(128)}, u32[]{:S(2)}) copy-start(f32[128]{0:T(128)} %param.13) | copy-start | bytes 1540
  6.5 249.8 %all-gather.3.cloned.1.call-start = ((), (), s32[]{:S(2)}) async-start(), calls=%async_computation.2 | async-start | bytes 4227072 | tf_op jit(solution)/shard_map/all_gather | solution.py:100
  16.2 6.3 %copy-start.11 = (bf16[128,2]{0,1:T(2,128)(2,1)S(1)}, bf16[128,2]{0,1:T(2,128)(2,1)}, u32[]{:S(2)}) copy-start(bf16[128,2]{0,1:T(2,128)(2,1)} %param.18) | copy-start | bytes 1540
  21.1 1.3 copy-start.2
  23.8 9.0 %copy-start.9 = (s32[16,16]{1,0:T(8,128)S(1)}, s32[16,16]{1,0:T(8,128)}, u32[]{:S(2)}) copy-start(s32[16,16]{1,0:T(8,128)} %param.20) | copy-start | bytes 3076
  23.8 62.6 %all-to-all-start = ((bf16[128,64,128]{2,0,1:T(8,128)(2,1)}), bf16[128,64,128]{2,0,1:T(8,128)(2,1)S(1)}, u32[]{:S(2)}, u32[]{:S(2)}) async-start(bf16[128,64,128]{2,0,1:T(8,128)(2,1)} %copy-done.2), calls=%async_computation | async-start | bytes 4194304 | tf_op jit(solution)/shard_map/all_to_all | solution.py:94
  86.4 0.7 copy-start.5
  86.6 2.4 copy-start.6
  89.0 0.9 copy-start.7
  89.8 0.9 copy-start.8
  262.9 7.3 %copy-start.4 = (s32[1024]{0:T(1024)S(1)}, s32[1024]{0:T(1024)}, u32[]{:S(2)}) copy-start(s32[1024]{0:T(1024)} %param.21) | copy-start | bytes 12292
  274.3 1.3 copy-start.3
  282.6 1.3 copy-start.3
  290.9 1.3 copy-start.3
  299.3 1.3 copy-start.3
  307.6 1.3 copy-start.3
  315.9 1.3 copy-start.3
  324.2 1.3 copy-start.3
  332.5 1.3 copy-start.3
  340.7 1.3 copy-start.3
  349.1 1.3 copy-start.3
  357.4 1.3 copy-start.3
  365.7 1.3 copy-start.3
  374.0 1.3 copy-start.3
  382.3 1.3 copy-start.3
  390.6 1.3 copy-start.3
  398.9 1.3 copy-start.3
  446.4 25.3 %collective-permute-start = (bf16[128,64,64]{0,2,1:T(8,128)(2,1)S(1)}, bf16[128,64,64]{0,2,1:T(8,128)(2,1)S(1)}, u32[]{:S(2)}, u32[]{:S(2)}) collective-permute-start(bf16[128,64,64]{0,2,1:T(8,128)(2,1)S(1)} %bitcast.117), channel_id=1, source_target_pairs={{0,1},{1,0},{2,3},{3,2},{4,5},{5,4},{6,7},{7,6},{8,9},{9,8},{10,11... | collective-permute-start | bytes 3145736 | tf_op jit(solution)/shard_map/ppermute | solution.py:16
Sparse Core Ops, SparseCore 0:
  23.9 232.4 all-gather.2
where the time goes:
time: 482 us; the launch traced here: 480 us
  waiting for transfers between devices  239 us (50%)
  matrix products  84.4 us (18%)
  other arithmetic  50.8 us (11%)
  local copies, waits for them, and re-layouts  36.5 us (8%)
  blocking collectives  32.9 us (7%)
  between operations  13.6 us (3%)
  starting transfers between devices  12.1 us (3%)
  loops' own time  10.9 us (2%)
    all_gather x1, waiting for transfers between devices, per_device(): lax.all_gather(bias_tile[None], ('row', 'col'), axis=0, tiled=True)  163 us
    all_to_all x1, waiting for transfers between devices, per_device(): lax.all_to_all(normed, 'row', split_axis=1, concat_axis=0, tiled=True)  53.6 us
    dot_general x16, matrix products, visit_keys(): jnp.einsum('jhqk,kjhd->jhqd', exponent.astype(jnp.bfloat16), values, pref...  46.3 us
    all_to_all x1, blocking collectives, per_device(): lax.all_to_all(gated_strip, 'row', split_axis=0, concat_axis=1, tiled=True)  32.9 us
    dot_general x16, matrix products, visit_keys(): jnp.einsum('qjhd,kjhd->jhqk', query, keys, preferred_element_type=jnp.flo...  22.6 us
    ppermute x1, waiting for transfers between devices, partner_2(): return lax.ppermute(value, axis, pairs)  21.6 us
    reduce_sum x16, other arithmetic, visit_keys(): running_sum = jnp.sum(exponent, axis=-1)  19.9 us
    transpose x16, other arithmetic, query_block(): jnp.transpose(lax.dynamic_slice_in_dim(bias_full, start, block_size, 1).a...  16 us
  transfers between devices with their start and end apart: 3, of which 3 were waited for; matrix products, arithmetic and copies ran while one was open for 1% of the time, Pallas kernels for 0%

commit v1 on v0

v1 whole, which is shorter than its diff:
```python
import math

import jax
import jax.numpy as jnp
from jax import lax
from jax.experimental import pallas as pl
from jax.experimental.pallas import tpu as pltpu
from jax.sharding import PartitionSpec as P

MESH = pl.DeviceIdType.MESH
F32 = jnp.float32
BF16 = jnp.bfloat16
VMEM = pltpu.VMEM
DMA = pltpu.SemaphoreType.DMA

epsilon = 1e-05
masked_score = -1000000000.0
LOG2E = math.log2(math.e)
SCALE = LOG2E / math.sqrt(32)
SAFE = 64.0
NT = (((1,), (1,)), ((), ()))


def ring(value, size):
    return lax.rem(value + size, size)


def spread_kernel(
    tile_ref, gain_in, wq_ref, wk_ref, wv_ref, wg_ref, wb_in, types_in, w_out_in, mask_in,
    qg_ref, kbd_ref, vbd_ref, bias_ref, bound_ref, mixing_ref, lists_ref,
    half, gain_ref, wb_ref, types_ref, w_out_ref, mask_ref, wide, send, strip, wbuf, wall, flat, bsend, tops,
    load_sem, col_send, col_recv, z_send, z_recv, w_send, w_recv,
    g_send, g_recv, s_send, s_recv, own_sem,
):
    row = lax.axis_index("row")
    col = lax.axis_index("col")
    head = lax.axis_index("head")
    core = lax.rem(col, 2)
    x = lax.rem(lax.div(col, 2), 4)
    y = head * 2 + lax.div(col, 8)

    def place(x_, y_, core_=None):
        return (row, lax.rem(y_, 2) * 8 + x_ * 2 + (core if core_ is None else core_), lax.div(y_, 2))

    def along_z(step):
        return (ring(row + step, 8), col, head)

    partner = place(x, ring(y + 2, 4))
    peers = [along_z(step) for step in range(1, 8)]
    peers += [place(ring(x + 1, 4), y), place(ring(x - 1, 4), y)]
    peers += [place(x, ring(y + 1, 4)), place(x, ring(y - 1, 4)), partner]
    peers += [place(x, y, 1 - core)]
    barrier = pltpu.get_barrier_semaphore()
    for peer in peers:
        pl.semaphore_signal(barrier, inc=1, device_id=peer, device_id_type=MESH)

    loads = [
        (tile_ref.at[:, pl.ds(pl.multiple_of(head * 32, 32), 32), :], half),
        (gain_in, gain_ref), (wb_in, wb_ref), (types_in, types_ref),
    ]
    loads += [
        (ref, wbuf.at[head, pl.ds(kind * 64, 64)]) for kind, ref in enumerate((wq_ref, wk_ref, wv_ref, wg_ref))
    ]
    loads += [(w_out_in, w_out_ref), (mask_in, mask_ref)]
    loads = [pltpu.make_async_copy(src, dst, load_sem.at[n]) for n, (src, dst) in enumerate(loads)]
    for load in loads:
        load.start()
    tops[...] = jnp.zeros_like(tops)
    for load in loads:
        load.wait()
    wbuf[head, 256:272, :] = jnp.concatenate(
        [wb_ref[...].astype(F32), jnp.zeros((14, 128), F32)], axis=0
    ).astype(BF16)

    def widen(block, carry):
        rows = half[pl.ds(block * 8, 8)].astype(F32).reshape(256, 128)
        wide[pl.ds(pl.multiple_of(block * 256, 256), 256), :] = rows
        return carry

    lax.fori_loop(0, 16, widen, 0)
    ones = jnp.ones((128, 128), BF16)
    gain = gain_ref[...]

    def norm_for(target, carry):
        for jj in range(4):
            value = wide[pl.ds(4 * target + jj, 128, stride=32), :]
            mean = jnp.dot(value.astype(BF16), ones, preferred_element_type=F32) * (1.0 / 128)
            centred = value - mean
            squares = (centred * centred).astype(BF16)
            spread = jnp.dot(squares, ones, preferred_element_type=F32) * (1.0 / 128)
            normed = centred * lax.rsqrt(spread + epsilon) * gain
            send[target, jj] = normed.astype(BF16)
        return carry

    lax.fori_loop(0, 4, norm_for, 0, unroll=2)
    pl.semaphore_wait(barrier, len(peers))
    w_copy = pltpu.make_async_remote_copy(
        src_ref=wbuf.at[head], dst_ref=wbuf.at[head], send_sem=w_send, recv_sem=w_recv,
        device_id=partner, device_id_type=MESH,
    )
    w_copy.start()
    lax.fori_loop(4, 8, norm_for, 0, unroll=2)
    pltpu.make_async_remote_copy(
        src_ref=wbuf.at[1 - head], dst_ref=wbuf.at[1 - head], send_sem=w_send, recv_sem=w_recv,
        device_id=partner, device_id_type=MESH,
    ).wait_recv()

    wb = wbuf[0, 256:272, :].astype(F32) + pltpu.roll(wbuf[1, 256:272, :].astype(F32), 2, 0)
    weighted = wb * gain
    wbt = wb.astype(BF16)

    def bias_for(target, carry):
        part = lax.dot_general(wbt, send[target].reshape(512, 128), NT, preferred_element_type=F32)
        for jj in range(4):
            flat[pl.ds(pl.multiple_of((4 * target + jj) * 8, 8), 8), :] = part[0:8, jj * 128:jj * 128 + 128]
        return carry

    lax.fori_loop(0, 8, bias_for, 0, unroll=4)
    living = jnp.broadcast_to(types_ref[pl.ds(row, 1), :] != 0, (32, 128))
    by_head = [
        jnp.where(living, flat[pl.ds(h, 32, stride=8), :] * LOG2E, masked_score) for h in range(4)
    ]
    bsend[0] = jnp.concatenate([b[:, :64] for b in by_head], axis=1).astype(BF16)
    bsend[1] = jnp.concatenate([b[:, 64:] for b in by_head], axis=1).astype(BF16)

    def unit(x_, y_, low, count, core_=None):
        return bias_ref.at[
            lax.rem(y_, 2), x_, core if core_ is None else core_, pl.ds(low, count), lax.div(y_, 2)
        ]

    sent = [w_copy]

    def push(src, dst, send_sem, recv_sem, device):
        copy = pltpu.make_async_remote_copy(
            src_ref=src, dst_ref=dst, send_sem=send_sem, recv_sem=recv_sem,
            device_id=device, device_id_type=MESH,
        )
        copy.start()
        sent.append(copy)

    def arrive(dst, send_sem, recv_sem):
        pltpu.make_async_remote_copy(
            src_ref=dst, dst_ref=dst, send_sem=send_sem, recv_sem=recv_sem,
            device_id=partner, device_id_type=MESH,
        ).wait_recv()

    def chunk(step, low=0, count=2):
        return unit(x, y, 2 * ring(row + step, 8) + low, count)

    def z_push(k, src, dst, step):
        push(src, dst, z_send.at[k], z_recv.at[k], along_z(step))

    def z_arrive(k, dst):
        arrive(dst, z_send.at[k], z_recv.at[k])

    own = pltpu.make_async_copy(bsend, chunk(0), own_sem.at[0])
    own.start()
    for k, step in enumerate((2, -2, 1, -1)):
        z_push(k, bsend, chunk(0), step)

    def strip_rows(step):
        source = ring(row + step, 8)
        return strip.at[:, pl.ds(pl.multiple_of(source * 128, 128), 128), :]

    def col_push(step):
        target = ring(row + step, 8)
        push(send.at[target], strip_rows(0), col_send.at[step], col_recv.at[step], along_z(step))

    own_cols = pltpu.make_async_copy(send.at[row], strip_rows(0), own_sem.at[1])
    own_cols.start()
    col_push(1)
    col_push(7)

    for kind, place_of in enumerate((1, 0, 2, 3)):
        for s in range(2):
            wall[place_of * 128 + s * 64:place_of * 128 + s * 64 + 64, :] = wbuf[s, kind * 64:kind * 64 + 64, :]
    together = (
        lax.div(lax.broadcasted_iota(jnp.int32, (128, 128), 0), 32)
        == lax.div(lax.broadcasted_iota(jnp.int32, (128, 128), 1), 32)
    ).astype(F32).astype(BF16)

    key_head = lax.div(lax.broadcasted_iota(jnp.int32, (128, 128), 0), 32)
    side_of = lax.div(lax.broadcasted_iota(jnp.int32, (128, 128), 1), 64)
    key_here = [(key_head == 2 * n + side_of).astype(F32).astype(BF16) for n in range(2)]
    lane_head = lax.div(lax.broadcasted_iota(jnp.int32, (64, 128), 1), 32)
    value_here = [(lane_head == h).astype(F32).astype(BF16) for h in range(4)]

    def project(step):
        source = ring(row + step, 8)
        rows = pl.ds(pl.multiple_of(source * 128, 128), 128)

        def one(jj, carry):
            value = strip[jj, rows, :]
            keys = lax.dot_general(wall[0:128, :], value, NT, preferred_element_type=F32)
            left = lax.dot_general(value, wall[128:256, :], NT, preferred_element_type=F32)
            right = lax.dot_general(value, wall[256:512, :], NT, preferred_element_type=F32)
            query = left * SCALE
            qg_ref[0, jj, rows, :] = query.astype(BF16)
            qg_ref[1, jj, rows, :] = jax.nn.sigmoid(right[:, 128:]).astype(BF16)
            short = keys.astype(BF16)
            values = right[:, :128].astype(BF16)
            for odd in range(2):
                twice = jnp.concatenate([short[:, odd * 64:odd * 64 + 64]] * 2, axis=1)
                for n in range(2):
                    kbd_ref[jj, 2 * source + odd, :, n * 128:(n + 1) * 128] = twice * key_here[n]
                for h in range(4):
                    vbd_ref[jj, 2 * source + odd, h * 64:(h + 1) * 64, :] = (
                        values[odd * 64:odd * 64 + 64, :] * value_here[h]
                    )
            lengths = jnp.dot((query * query).astype(BF16), together, preferred_element_type=F32)
            tops[0:1, :] = jnp.maximum(tops[0:1, :], jnp.max(lengths, axis=0, keepdims=True))
            lengths = jnp.dot(together, (keys * keys).astype(BF16), preferred_element_type=F32)
            tops[1:2, :] = jnp.maximum(tops[1:2, :], jnp.max(lengths, axis=0, keepdims=True))
            return carry

        lax.fori_loop(0, 4, one, 0, unroll=2)

    def take(step):
        arrive(strip_rows(-step), col_send.at[step], col_recv.at[step])
        project(-step)

    own.wait()
    own_cols.wait()
    for k, step in enumerate((-2, 2, -1, 1)):
        z_arrive(k, chunk(step))
    z_push(4, chunk(-2), chunk(-2), 1)
    z_push(5, chunk(2), chunk(2), -1)
    z_push(6, chunk(-2, 0, 1), chunk(-2, 0, 1), 2)
    z_push(7, chunk(2, 1, 1), chunk(2, 1, 1), -2)
    for step in (2, 6, 3, 5, 4):
        col_push(step)
    project(0)
    z_arrive(4, chunk(-3))
    z_arrive(5, chunk(3))
    z_arrive(6, chunk(4, 0, 1))
    z_arrive(7, chunk(4, 1, 1))

    def make_lists():
        mixing_ref[...] = w_out_ref[...].astype(F32).T.astype(BF16)
        part = mask_ref[...].astype(F32)
        diagonal = lax.broadcasted_iota(jnp.int32, (16, 16), 0) == lax.broadcasted_iota(jnp.int32, (16, 16), 1)
        part = jnp.where((part == 1.0) | diagonal, 1.0, 0.0)
        allowed = jnp.concatenate([part, jnp.zeros((16, 112), F32)], axis=1)
        before = [jnp.zeros((1, 128), F32)]
        for i in range(16):
            before.append(before[-1] + allowed[i:i + 1, :])
        rank = jnp.concatenate(before[:16], axis=0)
        pairs = jnp.broadcast_to(jnp.floor((before[16] + 1.0) * 0.5), (16, 128))
        earlier = (
            lax.broadcasted_iota(jnp.int32, (128, 128), 0) < lax.broadcasted_iota(jnp.int32, (128, 128), 1)
        ).astype(F32).astype(BF16)
        start = jnp.dot(pairs.astype(BF16), earlier, preferred_element_type=F32)
        total = jnp.sum(pairs[0:1, :], axis=1, keepdims=True)
        rank = rank + 2.0 * start
        entry = 2.0 * lax.broadcasted_iota(jnp.int32, (16, 128), 1).astype(F32)
        number = lax.broadcasted_iota(jnp.int32, (16, 128), 0).astype(F32)
        block = jnp.zeros((16, 128), F32)
        picked = [jnp.zeros((16, 128), F32)] * 2
        found = [jnp.zeros((16, 128), F32)] * 2
        for k in range(16):
            at = jnp.broadcast_to(rank[:, k:k + 1], (16, 128))
            here = jnp.broadcast_to(allowed[:, k:k + 1], (16, 128))
            for side in range(2):
                hit = jnp.where(at == entry + side, here, 0.0)
                found[side] = found[side] + hit
                picked[side] = picked[side] + hit * number
                if side == 0:
                    block = block + hit * k
        rows = [jnp.sum(block, axis=0, keepdims=True)]
        for side in range(2):
            missing = 1.0 - jnp.sum(found[side], axis=0, keepdims=True)
            rows.append(jnp.sum(picked[side], axis=0, keepdims=True) + (16.0 + side) * missing)
        rows.append(jnp.broadcast_to(total, (1, 128)))
        rows.append(jnp.zeros((4, 128), F32))
        lists_ref[...] = jnp.concatenate(rows, axis=0).astype(jnp.int32)

    def node(run, a, b):
        return (a, b) if run == 0 else (b, a)

    first = (x, y)
    second = (y, x)

    def shipment(run, index, a, b, low, count, to_a, to_b):
        k = run * 20 + index
        ref = unit(*node(run, a, b), run * 8 + low, count)
        push(ref, ref, g_send.at[k], g_recv.at[k], place(*node(run, to_a, to_b)))

    def receive(run, index, a, b, low, count):
        k = run * 20 + index
        arrive(unit(*node(run, a, b), run * 8 + low, count), g_send.at[k], g_recv.at[k])

    def to_sibling(run, u, v, a, b):
        k = run * 16 + u * 4 + v
        ref = unit(*node(run, a, b), run * 8, 8)
        push(ref, ref, s_send.at[k], s_recv.at[k], place(x, y, 1 - core))

    def across(run, u, a, b):
        shipment(run, 4 + 4 * u, a, b, 0, 8, first[run], ring(b + 1, 4))
        shipment(run, 5 + 4 * u, a, b, 0, 8, first[run], ring(b - 1, 4))

    for run in range(2):
        a, b = first[run], second[run]
        shipment(run, 0, a, b, 0, 8, ring(a + 1, 4), b)
        shipment(run, 1, a, b, 0, 8, ring(a - 1, 4), b)
    for run in range(2):
        a, b = first[run], second[run]
        across(run, 0, a, b)
        to_sibling(run, 0, 0, a, b)
    for run in range(2):
        a, b = first[run], second[run]
        receive(run, 0, ring(a - 1, 4), b, 0, 8)
        shipment(run, 2, ring(a - 1, 4), b, 0, 4, ring(a + 1, 4), b)
        receive(run, 1, ring(a + 1, 4), b, 0, 8)
        shipment(run, 3, ring(a + 1, 4), b, 4, 4, ring(a - 1, 4), b)
    for run in range(2):
        a, b = first[run], second[run]
        across(run, 1, ring(a - 1, 4), b)
        to_sibling(run, 1, 0, ring(a - 1, 4), b)
        across(run, 2, ring(a + 1, 4), b)
        to_sibling(run, 2, 0, ring(a + 1, 4), b)
    for run in range(2):
        a, b = first[run], second[run]
        receive(run, 2, ring(a + 2, 4), b, 0, 4)
        receive(run, 3, ring(a + 2, 4), b, 4, 4)
        across(run, 3, ring(a + 2, 4), b)
        to_sibling(run, 3, 0, ring(a + 2, 4), b)
    take(1)
    take(7)
    for u in range(4):
        for run in range(2):
            a, b = ring(first[run] + (0, -1, 1, 2)[u], 4), second[run]
            receive(run, 4 + 4 * u, a, ring(b - 1, 4), 0, 8)
            shipment(run, 6 + 4 * u, a, ring(b - 1, 4), 0, 4, first[run], ring(b + 1, 4))
            to_sibling(run, u, 1, a, ring(b - 1, 4))
            receive(run, 5 + 4 * u, a, ring(b + 1, 4), 0, 8)
            shipment(run, 7 + 4 * u, a, ring(b + 1, 4), 4, 4, first[run], ring(b - 1, 4))
            to_sibling(run, u, 2, a, ring(b + 1, 4))
        if u == 1:
            make_lists()
        if u == 3:
            take(2)
            take(6)
    for u in range(4):
        for run in range(2):
            a, b = ring(first[run] + (0, -1, 1, 2)[u], 4), second[run]
            receive(run, 6 + 4 * u, a, ring(b + 2, 4), 0, 4)
            receive(run, 7 + 4 * u, a, ring(b + 2, 4), 4, 4)
            to_sibling(run, u, 3, a, ring(b + 2, 4))
    for step in (3, 5, 4):
        take(step)
    bound_ref[0:8, :] = tops[...]
    bound_ref[8:24, :] = jnp.broadcast_to(jnp.sum(weighted * weighted, axis=1, keepdims=True), (16, 128))
    for run in range(2):
        for u in range(4):
            for v in range(4):
                a = ring(first[run] + (0, -1, 1, 2)[u], 4)
                b = ring(second[run] + (0, -1, 1, 2)[v], 4)
                k = run * 16 + u * 4 + v
                arrive(unit(*node(run, a, b), run * 8, 8, 1 - core), s_send.at[k], s_recv.at[k])
    for copy in sent:
        copy.wait_send()


def spread(*operands):
    whole = pl.BlockSpec(memory_space=VMEM)
    return pl.pallas_call(
        spread_kernel,
        out_shape=(
            jax.ShapeDtypeStruct((2, 4, 1024, 128), BF16),
            jax.ShapeDtypeStruct((4, 16, 128, 256), BF16),
            jax.ShapeDtypeStruct((4, 16, 256, 128), BF16),
            jax.ShapeDtypeStruct((2, 4, 2, 16, 2, 32, 256), BF16),
            jax.ShapeDtypeStruct((24, 128), F32),
            jax.ShapeDtypeStruct((128, 128), BF16),
            jax.ShapeDtypeStruct((8, 128), jnp.int32),
        ),
        in_specs=[pl.BlockSpec(memory_space=pltpu.HBM)] * len(operands),
        out_specs=(whole,) * 7,
        scratch_shapes=[
            VMEM((128, 32, 128), BF16),
            VMEM((1, 128), F32),
            VMEM((2, 128), BF16),
            VMEM((8, 128), jnp.int32),
            VMEM((128, 128), BF16),
            VMEM((16, 16), jnp.int32),
            VMEM((4096, 128), F32),
            VMEM((8, 4, 128, 128), BF16),
            VMEM((4, 1024, 128), BF16),
            VMEM((2, 272, 128), BF16),
            VMEM((512, 128), BF16),
            VMEM((256, 128), F32),
            VMEM((2, 32, 256), BF16),
            VMEM((8, 128), F32),
            DMA((10,)), DMA((8,)), DMA((8,)), DMA((8,)), DMA((8,)), DMA, DMA,
            DMA((40,)), DMA((40,)), DMA((32,)), DMA((32,)), DMA((2,)),
        ],
        compiler_params=pltpu.CompilerParams(
            collective_id=0, has_side_effects=True, vmem_limit_bytes=32 * 1024 * 1024
        ),
        name="spread",
    )(*operands)


def attend_kernel(
    lists_ref, qg_ref, kbd, vbd, bias, bound_ref,
    acc0, acc1, acc2, acc3,
    peak,
):
    accs = (acc0, acc1, acc2, acc3)
    for acc in accs:
        acc[...] = jnp.zeros_like(acc)
    same = (
        lax.div(lax.broadcasted_iota(jnp.int32, (256, 128), 0), 64)
        == lax.div(lax.broadcasted_iota(jnp.int32, (256, 128), 1), 32)
    ).astype(F32).astype(BF16)

    reach = jnp.sqrt(jnp.max(bound_ref[0:1, :])) * jnp.sqrt(jnp.max(bound_ref[1:2, :]))
    bias_reach = jnp.sqrt(jnp.max(bound_ref[8:24, :])) * (math.sqrt(128) * LOG2E)
    safe = (reach + bias_reach) * 1.03 <= SAFE

    def query(j, i):
        return qg_ref[0, j, pl.ds(pl.multiple_of(jnp.minimum(i, 15) * 64, 64), 64), :]

    def values_of(j, block):
        return jnp.concatenate([vbd[j, block], same], axis=1)

    total_pairs = lists_ref[3, 0]

    @pl.when(safe)
    def _():
        def step(t, carry):
            work = []
            for side in range(2):
                e = 2 * t + side
                block = lists_ref[0, e]
                ids = (lists_ref[1, e], lists_ref[2, e])
                offset = jnp.concatenate(
                    [bias[jnp.minimum(i, 15), block].astype(F32) for i in ids], axis=0
                )
                work.append((block, ids, offset))
            for j in range(4):
                for block, ids, offset in work:
                    queries = jnp.concatenate([query(j, i) for i in ids], axis=0)
                    score = jnp.dot(queries, kbd[j, block], preferred_element_type=F32)
                    weights = jnp.exp2(score + offset).astype(BF16)
                    total = jnp.dot(weights, values_of(j, block), preferred_element_type=F32)
                    olds = [accs[j][i] for i in ids]
                    for n in range(2):
                        accs[j][ids[n]] = olds[n] + total[n * 64:(n + 1) * 64, :]
            return carry

        lax.fori_loop(0, lax.div(total_pairs + 1, 2), step, 0)

    @pl.when(jnp.logical_not(safe))
    def _():
        peak[...] = jnp.full_like(peak, -1e30)

        def step(n, carry):
            e = lax.div(n, 2)
            block = lists_ref[0, e]
            i = lists_ref[1 + lax.rem(n, 2), e]
            offset = bias[jnp.minimum(i, 15), block].astype(F32)
            for j in range(4):
                score = jnp.dot(query(j, i), kbd[j, block], preferred_element_type=F32) + offset
                old = peak[j, i]
                tops = [
                    jnp.maximum(
                        jnp.max(score[:, h * 64:(h + 1) * 64], axis=1, keepdims=True),
                        old[:, h * 32:h * 32 + 1],
                    )
                    for h in range(4)
                ]
                shift = jnp.concatenate([jnp.broadcast_to(top, (64, 64)) for top in tops], axis=1)
                fresh = jnp.concatenate([jnp.broadcast_to(top, (64, 32)) for top in tops], axis=1)
                decay = jnp.exp2(old - fresh)
                weights = jnp.exp2(score - shift).astype(BF16)
                total = jnp.dot(weights, values_of(j, block), preferred_element_type=F32)
                accs[j][i] = accs[j][i] * jnp.concatenate([decay, decay], axis=1) + total
                peak[j, i] = fresh
            return carry

        lax.fori_loop(0, 2 * total_pairs, step, 0)


def attend(lists, qg, kbd, vbd, bias, bound):
    whole = pl.BlockSpec(memory_space=VMEM)
    return pl.pallas_call(
        attend_kernel,
        out_shape=[jax.ShapeDtypeStruct((18, 64, 256), F32)] * 4,
        in_specs=[pl.BlockSpec(memory_space=pltpu.SMEM)] + [whole] * 5,
        out_specs=[whole] * 4,
        scratch_shapes=[VMEM((4, 18, 64, 128), F32)],
        compiler_params=pltpu.CompilerParams(vmem_limit_bytes=24 * 1024 * 1024),
        name="attend",
    )(lists, qg, kbd, vbd, bias, bound)


def deliver_kernel(
    acc0, acc1, acc2, acc3, qg_ref, mixing_ref, out_ref, update_ref, send_sem, recv_sem, own_sem
):
    row = lax.axis_index("row")
    col = lax.axis_index("col")
    head = lax.axis_index("head")

    def other(flip):
        return (1 - head) if flip else head

    def device(step, flip):
        return (ring(row + step, 8), col, other(flip))

    moves = [(step, flip) for step in (4, 3, 5, 2, 6, 1, 7) for flip in (1, 0)] + [(0, 1)]
    barrier = pltpu.get_barrier_semaphore()
    for step, flip in moves:
        pl.semaphore_signal(barrier, inc=1, device_id=device(step, flip), device_id_type=MESH)

    def spot(step, flip):
        return out_ref.at[pl.ds((other(flip) * 8 + ring(row + step, 8)) * 4, 4)]

    def part(step, flip):
        return update_ref.at[other(flip), ring(row + step, 8)]

    def finish(step):
        target = ring(row + step, 8)
        rows = pl.ds(pl.multiple_of(target * 128, 128), 128)
        for j, acc in enumerate((acc0, acc1, acc2, acc3)):
            sums = acc[pl.ds(target * 2, 2)].reshape(128, 256)
            attention = sums[:, :128] / sums[:, 128:]
            gated = (attention * qg_ref[1, j, rows, :].astype(F32)).astype(BF16)
            update = lax.dot_general(mixing_ref[...], gated, NT, preferred_element_type=F32).astype(BF16)
            update_ref[0, target, j] = update[:64, :]
            update_ref[1, target, j] = update[64:, :]

    copies = []

    def push(step, flip):
        k = flip * 8 + step
        copy = pltpu.make_async_remote_copy(
            src_ref=part(step, flip), dst_ref=spot(0, 0),
            send_sem=send_sem.at[k], recv_sem=recv_sem.at[k],
            device_id=device(step, flip), device_id_type=MESH,
        )
        copy.start()
        copies.append(copy)

    for step in (4, 3, 5, 2, 6, 1, 7, 0):
        finish(step)
        if step == 4:
            pl.semaphore_wait(barrier, len(moves))
        push(step, 1)
        if step > 0:
            push(step, 0)
    own = pltpu.make_async_copy(part(0, 0), spot(0, 0), own_sem)
    own.start()
    own.wait()
    for step, flip in moves:
        k = flip * 8 + step
        pltpu.make_async_remote_copy(
            src_ref=spot(-step, flip), dst_ref=spot(-step, flip),
            send_sem=send_sem.at[k], recv_sem=recv_sem.at[k],
            device_id=device(step, flip), device_id_type=MESH,
        ).wait_recv()
    for copy in copies:
        copy.wait_send()


def deliver(accs, qg, mixing):
    whole = pl.BlockSpec(memory_space=VMEM)
    return pl.pallas_call(
        deliver_kernel,
        out_shape=jax.ShapeDtypeStruct((64, 64, 128), BF16),
        in_specs=[whole] * 6,
        out_specs=whole,
        scratch_shapes=[VMEM((2, 8, 4, 64, 128), BF16), DMA((16,)), DMA((16,)), DMA],
        compiler_params=pltpu.CompilerParams(
            collective_id=1, has_side_effects=True, vmem_limit_bytes=16 * 1024 * 1024
        ),
        name="deliver",
    )(*accs, qg, mixing)


def per_device(
    pair_field, ln_gain, w_query, w_key, w_value, w_gate, w_bias, w_out, tile_mask, type_ids
):
    weights = [w.T for w in (w_query, w_key, w_value, w_gate)]
    weights.append(w_bias.T)
    operands = (pair_field, ln_gain.reshape(1, 128), *weights, type_ids.reshape(8, 128), w_out, tile_mask)
    qg, kbd, vbd, bias, bound, mixing, lists = spread(
        *[pltpu.with_memory_space_constraint(operand, pltpu.HBM) for operand in operands]
    )
    accs = attend(lists, qg, kbd, vbd, bias.reshape(16, 16, 64, 256), bound)
    return jnp.transpose(deliver(accs, qg, mixing), (2, 0, 1))


def solution(mesh):
    return jax.shard_map(
        per_device,
        mesh=mesh,
        in_specs=(
            P("row", "col", None),
            P(),
            P(None, "head"),
            P(None, "head"),
            P(None, "head"),
            P(None, "head"),
            P(None, "head"),
            P(),
            P(),
            P(),
        ),
        out_specs=P("row", "col", "head"),
        check_vma=False,
    )
```

time: 482 us -> 170 us (0.35)
  waiting for transfers between devices: 239 us -> 0 us
  Pallas kernels: 0 us -> 169 us
  matrix products: 84.4 us -> 0 us
  other arithmetic: 50.8 us -> 0 us
  local copies, waits for them, and re-layouts: 36.5 us -> 0.97 us
  blocking collectives: 32.9 us -> 0 us
  between operations: 13.6 us -> 0.02 us
  starting transfers between devices: 12.1 us -> 0 us
  loops' own time: 10.9 us -> 0 us
    pallas_call x0 -> x3, Pallas kernels: none -> 169 us  [the longest x1 89.2 us: attend(): pl.pallas_call(attend_kernel, out_shape=[jax.ShapeDtypeStruct((18, 64, 25...]
    all_gather x1 -> x0, waiting for transfers between devices: 163 us -> none  [per_device(): lax.all_gather(bias_tile[None], ('row', 'col'), axis=0, tiled=True)]
    dot_general x55 -> x0, matrix products: 84.4 us -> none  [the longest x16 46.3 us: visit_keys(): jnp.einsum('jhqk,kjhd->jhqd', exponent.astype(jnp.bfloat16), values, pref...]
    all_to_all x1 -> x0, waiting for transfers between devices: 53.6 us -> none  [per_device(): lax.all_to_all(normed, 'row', split_axis=1, concat_axis=0, tiled=True)]
    all_to_all x1 -> x0, blocking collectives: 32.9 us -> none  [per_device(): lax.all_to_all(gated_strip, 'row', split_axis=0, concat_axis=1, tiled=True)]
    reduce_sum x18 -> x0, other arithmetic: 29.5 us -> none  [the longest x16 19.9 us: visit_keys(): running_sum = jnp.sum(exponent, axis=-1)]
    ppermute x1 -> x0, waiting for transfers between devices: 21.6 us -> none  [partner_2(): return lax.ppermute(value, axis, pairs)]
    transpose x16 -> x0, other arithmetic: 16 us -> none  [query_block(): jnp.transpose(lax.dynamic_slice_in_dim(bias_full, start, block_size, 1).a...]
  transfers between devices with their start and end apart: 3 -> 0, of which waited for: 3 -> 0; matrix products, arithmetic and copies ran while one was open for 1% -> 0% of each run, Pallas kernels for 0% -> 0%
where the time goes in v1:
time: 170 us
  Pallas kernels  169 us (99%)
    pallas_call x1, Pallas kernels, attend(): pl.pallas_call(attend_kernel, out_shape=[jax.ShapeDtypeStruct((18, 64, 25...  89.2 us
    pallas_call x1, Pallas kernels, spread(): pl.pallas_call(spread_kernel, out_shape=(jax.ShapeDtypeStruct((2, 4, 1024...  49.9 us
    pallas_call x1, Pallas kernels, deliver(): pl.pallas_call(deliver_kernel, out_shape=jax.ShapeDtypeStruct((64, 64, 12...  29.9 us

profile of v1, /device:TPU:1, one launch (start us, length us, event | category | flops | bytes accessed | tf_op | source)
XLA Modules:
  0.0 170.0 jit_solution(15089373394247698902)
XLA Ops:
  0.0 49.9 %spread.1 = (bf16[2,4,1024,128]{3,2,1,0:T(8,128)(2,1)S(1)}, bf16[4,16,128,256]{3,2,1,0:T(8,128)(2,1)S(1)}, bf16[4,16,256,128]{3,2,1,0:T(8,128)(2,1)S(1)}, bf16[2...) custom-call(bf16[128,64,128]{2,1,0:T(8,128)(2,1)} %tile_ref.1, ...), custom_call_target="tpu_custom_call" | custom-call | tf_op jit(solution)/shard_map/spread/pallas_call | solution.py:366
  49.9 89.2 %attend.1 = (f32[18,64,256]{2,1,0:T(8,128)S(1)}, f32[18,64,256]{2,1,0:T(8,128)S(1)}, f32[18,64,256]{2,1,0:T(8,128)S(1)}, f32[18,64,256]{2,1,0:T(8,128)S(1)}) custom-call(s32[8,128]{1,0:T(8,128)S(1)} %get-tuple-element.16.lists_ref, bf16[2,4,1024,128]{3,2,1,0:T(8,128)(2,1)S(1)} %get-tuple-element.17.qg_ref, ...), custom_call_target="tpu_custom_call" | custom-call | tf_op jit(solution)/shard_map/attend/pallas_call | solution.py:487
  139.1 29.9 %deliver.1 = bf16[64,64,128]{2,1,0:T(8,128)(2,1)S(1)} custom-call(f32[18,64,256]{2,1,0:T(8,128)S(1)} %get-tuple-element.22.acc0, f32[18,64,256]{2,1,0:T(8,128)S(1)} %get-tuple-element.23.acc1, f32[18,64,256]{2,1,0:T(8,128)S(1)} %get-tuple-element.24.acc2, f32[18,64,256]{2,1,0:T(8,128)S(1)} %get-tuple-element.25.acc3, ...), custom_call_target="tpu_custom_call" | custom-call | tf_op jit(solution)/shard_map/deliver/pallas_call | solution.py:568
  169.0 1.0 copy.12

commit v2 on v1

--- a/solution.py
+++ b/solution.py
@@ -81,7 +81,8 @@
     ones = jnp.ones((128, 128), BF16)
     gain = gain_ref[...]
 
-    def norm_for(target, carry):
+    def norm_for(step):
+        target = ring(row + step, 8)
         for jj in range(4):
             value = wide[pl.ds(4 * target + jj, 128, stride=32), :]
             mean = jnp.dot(value.astype(BF16), ones, preferred_element_type=F32) * (1.0 / 128)
@@ -90,16 +91,45 @@
             spread = jnp.dot(squares, ones, preferred_element_type=F32) * (1.0 / 128)
             normed = centred * lax.rsqrt(spread + epsilon) * gain
             send[target, jj] = normed.astype(BF16)
+
+    def norm_near(n, carry):
+        norm_for(n)
+        norm_for(-n)
         return carry
 
-    lax.fori_loop(0, 4, norm_for, 0, unroll=2)
+    def norm_far(n, carry):
+        norm_for(3 + n)
+        norm_for(-3 * (1 - n))
+        return carry
+
+    lax.fori_loop(1, 3, norm_near, 0)
     pl.semaphore_wait(barrier, len(peers))
     w_copy = pltpu.make_async_remote_copy(
         src_ref=wbuf.at[head], dst_ref=wbuf.at[head], send_sem=w_send, recv_sem=w_recv,
         device_id=partner, device_id_type=MESH,
     )
     w_copy.start()
-    lax.fori_loop(4, 8, norm_for, 0, unroll=2)
+    sent = [w_copy]
+
+    def push(src, dst, send_sem, recv_sem, device):
+        copy = pltpu.make_async_remote_copy(
+            src_ref=src, dst_ref=dst, send_sem=send_sem, recv_sem=recv_sem,
+            device_id=device, device_id_type=MESH,
+        )
+        copy.start()
+        sent.append(copy)
+
+    def strip_rows(step):
+        source = ring(row + step, 8)
+        return strip.at[:, pl.ds(pl.multiple_of(source * 128, 128), 128), :]
+
+    def col_push(step):
+        target = ring(row + step, 8)
+        push(send.at[target], strip_rows(0), col_send.at[step], col_recv.at[step], along_z(step))
+
+    col_push(1)
+    col_push(7)
+    lax.fori_loop(0, 2, norm_far, 0)
     pltpu.make_async_remote_copy(
         src_ref=wbuf.at[1 - head], dst_ref=wbuf.at[1 - head], send_sem=w_send, recv_sem=w_recv,
         device_id=partner, device_id_type=MESH,
@@ -128,16 +158,6 @@
             lax.rem(y_, 2), x_, core if core_ is None else core_, pl.ds(low, count), lax.div(y_, 2)
         ]
 
-    sent = [w_copy]
-
-    def push(src, dst, send_sem, recv_sem, device):
-        copy = pltpu.make_async_remote_copy(
-            src_ref=src, dst_ref=dst, send_sem=send_sem, recv_sem=recv_sem,
-            device_id=device, device_id_type=MESH,
-        )
-        copy.start()
-        sent.append(copy)
-
     def arrive(dst, send_sem, recv_sem):
         pltpu.make_async_remote_copy(
             src_ref=dst, dst_ref=dst, send_sem=send_sem, recv_sem=recv_sem,
@@ -158,18 +178,8 @@
     for k, step in enumerate((2, -2, 1, -1)):
         z_push(k, bsend, chunk(0), step)
 
-    def strip_rows(step):
-        source = ring(row + step, 8)
-        return strip.at[:, pl.ds(pl.multiple_of(source * 128, 128), 128), :]
-
-    def col_push(step):
-        target = ring(row + step, 8)
-        push(send.at[target], strip_rows(0), col_send.at[step], col_recv.at[step], along_z(step))
-
     own_cols = pltpu.make_async_copy(send.at[row], strip_rows(0), own_sem.at[1])
     own_cols.start()
-    col_push(1)
-    col_push(7)
 
     for kind, place_of in enumerate((1, 0, 2, 3)):
         for s in range(2):
@@ -227,8 +237,6 @@
     z_push(5, chunk(2), chunk(2), -1)
     z_push(6, chunk(-2, 0, 1), chunk(-2, 0, 1), 2)
     z_push(7, chunk(2, 1, 1), chunk(2, 1, 1), -2)
-    for step in (2, 6, 3, 5, 4):
-        col_push(step)
     project(0)
     z_arrive(4, chunk(-3))
     z_arrive(5, chunk(3))
@@ -306,6 +314,8 @@
         a, b = first[run], second[run]
         across(run, 0, a, b)
         to_sibling(run, 0, 0, a, b)
+    for step in (2, 6, 3, 5, 4):
+        col_push(step)
     for run in range(2):
         a, b = first[run], second[run]
         receive(run, 0, ring(a - 1, 4), b, 0, 8)
@@ -542,10 +552,12 @@
         copy.start()
         copies.append(copy)
 
+    for step in (4, 3, 5):
+        finish(step)
+    pl.semaphore_wait(barrier, len(moves))
     for step in (4, 3, 5, 2, 6, 1, 7, 0):
-        finish(step)
-        if step == 4:
-            pl.semaphore_wait(barrier, len(moves))
+        if step not in (4, 3, 5):
+            finish(step)
         push(step, 1)
         if step > 0:
             push(step, 0)

time: 170 us -> 160 us (0.941)
  Pallas kernels: 169 us -> 159 us
    pallas_call x1, Pallas kernels: 89.2 us -> 81.9 us  [attend(): pl.pallas_call(attend_kernel, out_shape=[jax.ShapeDtypeStruct((18, 64, 25...]
    pallas_call x1, Pallas kernels: 49.9 us -> 48.1 us  [spread(): pl.pallas_call(spread_kernel, out_shape=(jax.ShapeDtypeStruct((2, 4, 1024...]
where the time goes in v2:
time: 160 us
  Pallas kernels  159 us (99%)
    pallas_call x1, Pallas kernels, attend(): pl.pallas_call(attend_kernel, out_shape=[jax.ShapeDtypeStruct((18, 64, 25...  81.9 us
    pallas_call x1, Pallas kernels, spread(): pl.pallas_call(spread_kernel, out_shape=(jax.ShapeDtypeStruct((2, 4, 1024...  48.1 us
    pallas_call x1, Pallas kernels, deliver(): pl.pallas_call(deliver_kernel, out_shape=jax.ShapeDtypeStruct((64, 64, 12...  28.6 us

profile of v2, /device:TPU:1, one launch (start us, length us, event | category | flops | bytes accessed | tf_op | source)
XLA Modules:
  0.0 159.5 jit_solution(16565379882128056327)
XLA Ops:
  0.0 48.1 %spread.1 = (bf16[2,4,1024,128]{3,2,1,0:T(8,128)(2,1)S(1)}, bf16[4,16,128,256]{3,2,1,0:T(8,128)(2,1)S(1)}, bf16[4,16,256,128]{3,2,1,0:T(8,128)(2,1)S(1)}, bf16[2...) custom-call(bf16[128,64,128]{2,1,0:T(8,128)(2,1)} %tile_ref.1, ...), custom_call_target="tpu_custom_call" | custom-call | tf_op jit(solution)/shard_map/spread/pallas_call | solution.py:376
  48.1 81.9 %attend.1 = (f32[18,64,256]{2,1,0:T(8,128)S(1)}, f32[18,64,256]{2,1,0:T(8,128)S(1)}, f32[18,64,256]{2,1,0:T(8,128)S(1)}, f32[18,64,256]{2,1,0:T(8,128)S(1)}) custom-call(s32[8,128]{1,0:T(8,128)S(1)} %get-tuple-element.16.lists_ref, bf16[2,4,1024,128]{3,2,1,0:T(8,128)(2,1)S(1)} %get-tuple-element.17.qg_ref, ...), custom_call_target="tpu_custom_call" | custom-call | tf_op jit(solution)/shard_map/attend/pallas_call | solution.py:497
  129.9 28.6 %deliver.1 = bf16[64,64,128]{2,1,0:T(8,128)(2,1)S(1)} custom-call(f32[18,64,256]{2,1,0:T(8,128)S(1)} %get-tuple-element.22.acc0, f32[18,64,256]{2,1,0:T(8,128)S(1)} %get-tuple-element.23.acc1, f32[18,64,256]{2,1,0:T(8,128)S(1)} %get-tuple-element.24.acc2, f32[18,64,256]{2,1,0:T(8,128)S(1)} %get-tuple-element.25.acc3, ...), custom_call_target="tpu_custom_call" | custom-call | tf_op jit(solution)/shard_map/deliver/pallas_call | solution.py:580
  158.6 1.0 copy.12

commit v3 on v2

--- a/solution.py
+++ b/solution.py
@@ -66,11 +66,7 @@
     for load in loads:
         load.start()
     tops[...] = jnp.zeros_like(tops)
-    for load in loads:
-        load.wait()
-    wbuf[head, 256:272, :] = jnp.concatenate(
-        [wb_ref[...].astype(F32), jnp.zeros((14, 128), F32)], axis=0
-    ).astype(BF16)
+    loads[0].wait()
 
     def widen(block, carry):
         rows = half[pl.ds(block * 8, 8)].astype(F32).reshape(256, 128)
@@ -79,6 +75,7 @@
 
     lax.fori_loop(0, 16, widen, 0)
     ones = jnp.ones((128, 128), BF16)
+    loads[1].wait()
     gain = gain_ref[...]
 
     def norm_for(step):
@@ -103,6 +100,11 @@
         return carry
 
     lax.fori_loop(1, 3, norm_near, 0)
+    for load in loads[2:]:
+        load.wait()
+    wbuf[head, 256:272, :] = jnp.concatenate(
+        [wb_ref[...].astype(F32), jnp.zeros((14, 128), F32)], axis=0
+    ).astype(BF16)
     pl.semaphore_wait(barrier, len(peers))
     w_copy = pltpu.make_async_remote_copy(
         src_ref=wbuf.at[head], dst_ref=wbuf.at[head], send_sem=w_send, recv_sem=w_recv,
@@ -164,8 +166,11 @@
             device_id=partner, device_id_type=MESH,
         ).wait_recv()
 
+    def slot(step):
+        return 2 * step - 1 if step > 0 else -2 * step
+
     def chunk(step, low=0, count=2):
-        return unit(x, y, 2 * ring(row + step, 8) + low, count)
+        return unit(x, y, 2 * slot(step) + low, count)
 
     def z_push(k, src, dst, step):
         push(src, dst, z_send.at[k], z_recv.at[k], along_z(step))
@@ -176,7 +181,7 @@
     own = pltpu.make_async_copy(bsend, chunk(0), own_sem.at[0])
     own.start()
     for k, step in enumerate((2, -2, 1, -1)):
-        z_push(k, bsend, chunk(0), step)
+        z_push(k, bsend, chunk(-step), step)
 
     own_cols = pltpu.make_async_copy(send.at[row], strip_rows(0), own_sem.at[1])
     own_cols.start()
@@ -197,6 +202,7 @@
 
     def project(step):
         source = ring(row + step, 8)
+        first_block = 2 * slot(step)
         rows = pl.ds(pl.multiple_of(source * 128, 128), 128)
 
         def one(jj, carry):
@@ -212,9 +218,9 @@
             for odd in range(2):
                 twice = jnp.concatenate([short[:, odd * 64:odd * 64 + 64]] * 2, axis=1)
                 for n in range(2):
-                    kbd_ref[jj, 2 * source + odd, :, n * 128:(n + 1) * 128] = twice * key_here[n]
+                    kbd_ref[jj, first_block + odd, :, n * 128:(n + 1) * 128] = twice * key_here[n]
                 for h in range(4):
-                    vbd_ref[jj, 2 * source + odd, h * 64:(h + 1) * 64, :] = (
+                    vbd_ref[jj, first_block + odd, h * 64:(h + 1) * 64, :] = (
                         values[odd * 64:odd * 64 + 64, :] * value_here[h]
                     )
             lengths = jnp.dot((query * query).astype(BF16), together, preferred_element_type=F32)
@@ -226,29 +232,35 @@
         lax.fori_loop(0, 4, one, 0, unroll=2)
 
     def take(step):
-        arrive(strip_rows(-step), col_send.at[step], col_recv.at[step])
-        project(-step)
+        arrive(strip_rows(step), col_send.at[(8 - step) % 8], col_recv.at[(8 - step) % 8])
+        project(step)
 
     own.wait()
     own_cols.wait()
     for k, step in enumerate((-2, 2, -1, 1)):
         z_arrive(k, chunk(step))
-    z_push(4, chunk(-2), chunk(-2), 1)
-    z_push(5, chunk(2), chunk(2), -1)
-    z_push(6, chunk(-2, 0, 1), chunk(-2, 0, 1), 2)
-    z_push(7, chunk(2, 1, 1), chunk(2, 1, 1), -2)
-    project(0)
-    z_arrive(4, chunk(-3))
-    z_arrive(5, chunk(3))
-    z_arrive(6, chunk(4, 0, 1))
-    z_arrive(7, chunk(4, 1, 1))
+    z_push(4, chunk(-2), chunk(-3), 1)
+    z_push(5, chunk(2), chunk(3), -1)
+    z_push(6, chunk(-2, 0, 1), chunk(4, 0, 1), 2)
+    z_push(7, chunk(2, 1, 1), chunk(4, 1, 1), -2)
+
+    def far_bias():
+        z_arrive(4, chunk(-3))
+        z_arrive(5, chunk(3))
+        z_arrive(6, chunk(4, 0, 1))
+        z_arrive(7, chunk(4, 1, 1))
 
     def make_lists():
         mixing_ref[...] = w_out_ref[...].astype(F32).T.astype(BF16)
         part = mask_ref[...].astype(F32)
+        place_ = lax.div(lax.broadcasted_iota(jnp.int32, (16, 128), 1), 2)
+        away = lax.div(place_ + 1, 2) * (2 * lax.rem(place_, 2) - 1)
+        there = 2 * lax.rem(row + away + 8, 8) + lax.rem(lax.broadcasted_iota(jnp.int32, (16, 128), 1), 2)
+        inside = lax.broadcasted_iota(jnp.int32, (16, 128), 1) < 16
+        turned = (inside & (lax.broadcasted_iota(jnp.int32, (16, 128), 0) == there)).astype(F32).astype(BF16)
         diagonal = lax.broadcasted_iota(jnp.int32, (16, 16), 0) == lax.broadcasted_iota(jnp.int32, (16, 16), 1)
         part = jnp.where((part == 1.0) | diagonal, 1.0, 0.0)
-        allowed = jnp.concatenate([part, jnp.zeros((16, 112), F32)], axis=1)
+        allowed = jnp.dot(part.astype(BF16), turned, preferred_element_type=F32)
         before = [jnp.zeros((1, 128), F32)]
         for i in range(16):
             before.append(before[-1] + allowed[i:i + 1, :])
@@ -308,13 +320,17 @@
 
     for run in range(2):
         a, b = first[run], second[run]
+        if run == 1:
+            project(0)
+            far_bias()
         shipment(run, 0, a, b, 0, 8, ring(a + 1, 4), b)
         shipment(run, 1, a, b, 0, 8, ring(a - 1, 4), b)
-    for run in range(2):
-        a, b = first[run], second[run]
         across(run, 0, a, b)
         to_sibling(run, 0, 0, a, b)
-    for step in (2, 6, 3, 5, 4):
+        if run == 0:
+            col_push(2)
+            col_push(6)
+    for step in (3, 5, 4):
         col_push(step)
     for run in range(2):
         a, b = first[run], second[run]
@@ -335,7 +351,7 @@
         across(run, 3, ring(a + 2, 4), b)
         to_sibling(run, 3, 0, ring(a + 2, 4), b)
     take(1)
-    take(7)
+    take(-1)
     for u in range(4):
         for run in range(2):
             a, b = ring(first[run] + (0, -1, 1, 2)[u], 4), second[run]
@@ -349,15 +365,16 @@
             make_lists()
         if u == 3:
             take(2)
-            take(6)
+            take(-2)
     for u in range(4):
         for run in range(2):
             a, b = ring(first[run] + (0, -1, 1, 2)[u], 4), second[run]
             receive(run, 6 + 4 * u, a, ring(b + 2, 4), 0, 4)
             receive(run, 7 + 4 * u, a, ring(b + 2, 4), 4, 4)
             to_sibling(run, u, 3, a, ring(b + 2, 4))
-    for step in (3, 5, 4):
-        take(step)
+        if u >= 2:
+            take((3, -3)[u - 2])
+    take(4)
     bound_ref[0:8, :] = tops[...]
     bound_ref[8:24, :] = jnp.broadcast_to(jnp.sum(weighted * weighted, axis=1, keepdims=True), (16, 128))
     for run in range(2):

time: 160 us -> 189 us (1.18)
  Pallas kernels: 159 us -> 188 us
    pallas_call x1, Pallas kernels: 81.9 us -> 111 us  [attend(): pl.pallas_call(attend_kernel, out_shape=[jax.ShapeDtypeStruct((18, 64, 25...]
where the time goes in v3:
time: 189 us
  Pallas kernels  188 us (99%)
    pallas_call x1, Pallas kernels, attend(): pl.pallas_call(attend_kernel, out_shape=[jax.ShapeDtypeStruct((18, 64, 25...  111 us
    pallas_call x1, Pallas kernels, spread(): pl.pallas_call(spread_kernel, out_shape=(jax.ShapeDtypeStruct((2, 4, 1024...  47.5 us
    pallas_call x1, Pallas kernels, deliver(): pl.pallas_call(deliver_kernel, out_shape=jax.ShapeDtypeStruct((64, 64, 12...  29.8 us

profile of v3, /device:TPU:1, one launch (start us, length us, event | category | flops | bytes accessed | tf_op | source)
XLA Modules:
  0.0 189.4 jit_solution(2892973099288075689)
XLA Ops:
  0.0 47.5 %spread.1 = (bf16[2,4,1024,128]{3,2,1,0:T(8,128)(2,1)S(1)}, bf16[4,16,128,256]{3,2,1,0:T(8,128)(2,1)S(1)}, bf16[4,16,256,128]{3,2,1,0:T(8,128)(2,1)S(1)}, bf16[2...) custom-call(bf16[128,64,128]{2,1,0:T(8,128)(2,1)} %tile_ref.1, ...), custom_call_target="tpu_custom_call" | custom-call | tf_op jit(solution)/shard_map/spread/pallas_call | solution.py:393
  47.5 111.2 %attend.1 = (f32[18,64,256]{2,1,0:T(8,128)S(1)}, f32[18,64,256]{2,1,0:T(8,128)S(1)}, f32[18,64,256]{2,1,0:T(8,128)S(1)}, f32[18,64,256]{2,1,0:T(8,128)S(1)}) custom-call(s32[8,128]{1,0:T(8,128)S(1)} %get-tuple-element.16.lists_ref, bf16[2,4,1024,128]{3,2,1,0:T(8,128)(2,1)S(1)} %get-tuple-element.17.qg_ref, ...), custom_call_target="tpu_custom_call" | custom-call | tf_op jit(solution)/shard_map/attend/pallas_call | solution.py:514
  158.7 29.8 %deliver.1 = bf16[64,64,128]{2,1,0:T(8,128)(2,1)S(1)} custom-call(f32[18,64,256]{2,1,0:T(8,128)S(1)} %get-tuple-element.22.acc0, f32[18,64,256]{2,1,0:T(8,128)S(1)} %get-tuple-element.23.acc1, f32[18,64,256]{2,1,0:T(8,128)S(1)} %get-tuple-element.24.acc2, f32[18,64,256]{2,1,0:T(8,128)S(1)} %get-tuple-element.25.acc3, ...), custom_call_target="tpu_custom_call" | custom-call | tf_op jit(solution)/shard_map/deliver/pallas_call | solution.py:597
  188.4 1.0 copy.12

commit v4 on v3

--- a/solution.py
+++ b/solution.py
@@ -157,7 +157,7 @@
 
     def unit(x_, y_, low, count, core_=None):
         return bias_ref.at[
-            lax.rem(y_, 2), x_, core if core_ is None else core_, pl.ds(low, count), lax.div(y_, 2)
+            low // 8, lax.rem(y_, 2), x_, core if core_ is None else core_, lax.div(y_, 2), pl.ds(low % 8, count)
         ]
 
     def arrive(dst, send_sem, recv_sem):
@@ -396,7 +396,7 @@
             jax.ShapeDtypeStruct((2, 4, 1024, 128), BF16),
             jax.ShapeDtypeStruct((4, 16, 128, 256), BF16),
             jax.ShapeDtypeStruct((4, 16, 256, 128), BF16),
-            jax.ShapeDtypeStruct((2, 4, 2, 16, 2, 32, 256), BF16),
+            jax.ShapeDtypeStruct((2, 2, 4, 2, 2, 8, 32, 256), BF16),
             jax.ShapeDtypeStruct((24, 128), F32),
             jax.ShapeDtypeStruct((128, 128), BF16),
             jax.ShapeDtypeStruct((8, 128), jnp.int32),
@@ -451,6 +451,11 @@
     def values_of(j, block):
         return jnp.concatenate([vbd[j, block], same], axis=1)
 
+    def offset_of(i, block):
+        at = (lax.div(block, 8), jnp.minimum(i, 15))
+        n = lax.rem(block, 8)
+        return [bias[at[0], at[1], half, n].astype(F32) for half in range(2)]
+
     total_pairs = lists_ref[3, 0]
 
     @pl.when(safe)
@@ -461,9 +466,7 @@
                 e = 2 * t + side
                 block = lists_ref[0, e]
                 ids = (lists_ref[1, e], lists_ref[2, e])
-                offset = jnp.concatenate(
-                    [bias[jnp.minimum(i, 15), block].astype(F32) for i in ids], axis=0
-                )
+                offset = jnp.concatenate(offset_of(ids[0], block) + offset_of(ids[1], block), axis=0)
                 work.append((block, ids, offset))
             for j in range(4):
                 for block, ids, offset in work:
@@ -486,7 +489,7 @@
             e = lax.div(n, 2)
             block = lists_ref[0, e]
             i = lists_ref[1 + lax.rem(n, 2), e]
-            offset = bias[jnp.minimum(i, 15), block].astype(F32)
+            offset = jnp.concatenate(offset_of(i, block), axis=0)
             for j in range(4):
                 score = jnp.dot(query(j, i), kbd[j, block], preferred_element_type=F32) + offset
                 old = peak[j, i]
@@ -616,7 +619,7 @@
     qg, kbd, vbd, bias, bound, mixing, lists = spread(
         *[pltpu.with_memory_space_constraint(operand, pltpu.HBM) for operand in operands]
     )
-    accs = attend(lists, qg, kbd, vbd, bias.reshape(16, 16, 64, 256), bound)
+    accs = attend(lists, qg, kbd, vbd, bias.reshape(2, 16, 2, 8, 32, 256), bound)
     return jnp.transpose(deliver(accs, qg, mixing), (2, 0, 1))
 
 

time: 189 us -> 164 us (0.87)
  Pallas kernels: 188 us -> 163 us
    pallas_call x1, Pallas kernels: 111 us -> 85.5 us  [attend(): pl.pallas_call(attend_kernel, out_shape=[jax.ShapeDtypeStruct((18, 64, 25...]
where the time goes in v4:
time: 164 us
  Pallas kernels  163 us (99%)
    pallas_call x1, Pallas kernels, attend(): pl.pallas_call(attend_kernel, out_shape=[jax.ShapeDtypeStruct((18, 64, 25...  85.5 us
    pallas_call x1, Pallas kernels, spread(): pl.pallas_call(spread_kernel, out_shape=(jax.ShapeDtypeStruct((2, 4, 1024...  47.5 us
    pallas_call x1, Pallas kernels, deliver(): pl.pallas_call(deliver_kernel, out_shape=jax.ShapeDtypeStruct((64, 64, 12...  29.8 us

profile of v4, /device:TPU:1, one launch (start us, length us, event | category | flops | bytes accessed | tf_op | source)
XLA Modules:
  0.0 163.8 jit_solution(5953350345408279668)
XLA Ops:
  0.0 47.5 %spread.1 = (bf16[2,4,1024,128]{3,2,1,0:T(8,128)(2,1)S(1)}, bf16[4,16,128,256]{3,2,1,0:T(8,128)(2,1)S(1)}, bf16[4,16,256,128]{3,2,1,0:T(8,128)(2,1)S(1)}, bf16[2...) custom-call(bf16[128,64,128]{2,1,0:T(8,128)(2,1)} %tile_ref.1, ...), custom_call_target="tpu_custom_call" | custom-call | tf_op jit(solution)/shard_map/spread/pallas_call | solution.py:393
  47.5 85.5 %attend.1 = (f32[18,64,256]{2,1,0:T(8,128)S(1)}, f32[18,64,256]{2,1,0:T(8,128)S(1)}, f32[18,64,256]{2,1,0:T(8,128)S(1)}, f32[18,64,256]{2,1,0:T(8,128)S(1)}) custom-call(s32[8,128]{1,0:T(8,128)S(1)} %get-tuple-element.16.lists_ref, bf16[2,4,1024,128]{3,2,1,0:T(8,128)(2,1)S(1)} %get-tuple-element.17.qg_ref, ...), custom_call_target="tpu_custom_call" | custom-call | tf_op jit(solution)/shard_map/attend/pallas_call | solution.py:517
  133.0 29.8 %deliver.1 = bf16[64,64,128]{2,1,0:T(8,128)(2,1)S(1)} custom-call(f32[18,64,256]{2,1,0:T(8,128)S(1)} %get-tuple-element.22.acc0, f32[18,64,256]{2,1,0:T(8,128)S(1)} %get-tuple-element.23.acc1, f32[18,64,256]{2,1,0:T(8,128)S(1)} %get-tuple-element.24.acc2, f32[18,64,256]{2,1,0:T(8,128)S(1)} %get-tuple-element.25.acc3, ...), custom_call_target="tpu_custom_call" | custom-call | tf_op jit(solution)/shard_map/deliver/pallas_call | solution.py:600
  162.8 1.0 copy.12

commit v5 on v4

--- a/solution.py
+++ b/solution.py
@@ -121,9 +121,11 @@
         copy.start()
         sent.append(copy)
 
-    def strip_rows(step):
+    def strip_rows(step, core_=None):
         source = ring(row + step, 8)
-        return strip.at[:, pl.ds(pl.multiple_of(source * 128, 128), 128), :]
+        return strip.at[
+            core if core_ is None else core_, :, pl.ds(pl.multiple_of(source * 128, 128), 128), :
+        ]
 
     def col_push(step):
         target = ring(row + step, 8)
@@ -155,10 +157,8 @@
     bsend[0] = jnp.concatenate([b[:, :64] for b in by_head], axis=1).astype(BF16)
     bsend[1] = jnp.concatenate([b[:, 64:] for b in by_head], axis=1).astype(BF16)
 
-    def unit(x_, y_, low, count, core_=None):
-        return bias_ref.at[
-            low // 8, lax.rem(y_, 2), x_, core if core_ is None else core_, lax.div(y_, 2), pl.ds(low % 8, count)
-        ]
+    def unit(x_, y_, low, count):
+        return bias_ref.at[low // 8, lax.rem(y_, 2), x_, lax.div(y_, 2), pl.ds(low % 8, count)]
 
     def arrive(dst, send_sem, recv_sem):
         pltpu.make_async_remote_copy(
@@ -186,7 +186,7 @@
     own_cols = pltpu.make_async_copy(send.at[row], strip_rows(0), own_sem.at[1])
     own_cols.start()
 
-    for kind, place_of in enumerate((1, 0, 2, 3)):
+    for kind, place_of in enumerate((2, 0, 1, 3)):
         for s in range(2):
             wall[place_of * 128 + s * 64:place_of * 128 + s * 64 + 64, :] = wbuf[s, kind * 64:kind * 64 + 64, :]
     together = (
@@ -200,27 +200,29 @@
     lane_head = lax.div(lax.broadcasted_iota(jnp.int32, (64, 128), 1), 32)
     value_here = [(lane_head == h).astype(F32).astype(BF16) for h in range(4)]
 
-    def project(step):
+    def project(core_, step):
         source = ring(row + step, 8)
         first_block = 2 * slot(step)
         rows = pl.ds(pl.multiple_of(source * 128, 128), 128)
+        own_rows = pl.ds(pl.multiple_of(source * 128 + core * 64, 64), 64)
+        into = pl.ds(pl.multiple_of(source * 64, 64), 64)
 
         def one(jj, carry):
-            value = strip[jj, rows, :]
+            m = core_ * 4 + jj
+            value = strip[core_, jj, rows, :]
             keys = lax.dot_general(wall[0:128, :], value, NT, preferred_element_type=F32)
-            left = lax.dot_general(value, wall[128:256, :], NT, preferred_element_type=F32)
-            right = lax.dot_general(value, wall[256:512, :], NT, preferred_element_type=F32)
-            query = left * SCALE
-            qg_ref[0, jj, rows, :] = query.astype(BF16)
-            qg_ref[1, jj, rows, :] = jax.nn.sigmoid(right[:, 128:]).astype(BF16)
+            values = lax.dot_general(value, wall[128:256, :], NT, preferred_element_type=F32).astype(BF16)
+            both = lax.dot_general(strip[core_, jj, own_rows, :], wall[256:512, :], NT, preferred_element_type=F32)
+            query = both[:, :128] * SCALE
+            qg_ref[0, m, into, :] = query.astype(BF16)
+            qg_ref[1, m, into, :] = jax.nn.sigmoid(both[:, 128:]).astype(BF16)
             short = keys.astype(BF16)
-            values = right[:, :128].astype(BF16)
             for odd in range(2):
                 twice = jnp.concatenate([short[:, odd * 64:odd * 64 + 64]] * 2, axis=1)
                 for n in range(2):
-                    kbd_ref[jj, first_block + odd, :, n * 128:(n + 1) * 128] = twice * key_here[n]
+                    kbd_ref[m, first_block + odd, :, n * 128:(n + 1) * 128] = twice * key_here[n]
                 for h in range(4):
-                    vbd_ref[jj, first_block + odd, h * 64:(h + 1) * 64, :] = (
+                    vbd_ref[m, first_block + odd, h * 64:(h + 1) * 64, :] = (
                         values[odd * 64:odd * 64 + 64, :] * value_here[h]
                     )
             lengths = jnp.dot((query * query).astype(BF16), together, preferred_element_type=F32)
@@ -231,18 +233,31 @@
 
         lax.fori_loop(0, 4, one, 0, unroll=2)
 
+    def share(step):
+        k = step % 8
+        push(strip_rows(step), strip_rows(step), s_send.at[k], s_recv.at[k], place(x, y, 1 - core))
+
     def take(step):
         arrive(strip_rows(step), col_send.at[(8 - step) % 8], col_recv.at[(8 - step) % 8])
-        project(step)
-
+        share(step)
+        project(core, step)
+
+    def take_shared(step):
+        k = step % 8
+        arrive(strip_rows(step, 1 - core), s_send.at[k], s_recv.at[k])
+        project(1 - core, step)
+
+    own_cols.wait()
+    share(0)
     own.wait()
-    own_cols.wait()
     for k, step in enumerate((-2, 2, -1, 1)):
         z_arrive(k, chunk(step))
     z_push(4, chunk(-2), chunk(-3), 1)
     z_push(5, chunk(2), chunk(3), -1)
     z_push(6, chunk(-2, 0, 1), chunk(4, 0, 1), 2)
     z_push(7, chunk(2, 1, 1), chunk(4, 1, 1), -2)
+    for step in (2, 6, 3, 5, 4):
+        col_push(step)
 
     def far_bias():
         z_arrive(4, chunk(-3))
@@ -260,6 +275,9 @@
         turned = (inside & (lax.broadcasted_iota(jnp.int32, (16, 128), 0) == there)).astype(F32).astype(BF16)
         diagonal = lax.broadcasted_iota(jnp.int32, (16, 16), 0) == lax.broadcasted_iota(jnp.int32, (16, 16), 1)
         part = jnp.where((part == 1.0) | diagonal, 1.0, 0.0)
+        wanted = lax.broadcasted_iota(jnp.int32, (16, 16), 0)
+        mine = (wanted < 8) & (lax.broadcasted_iota(jnp.int32, (16, 16), 1) == 2 * wanted + core)
+        part = jnp.dot(mine.astype(F32).astype(BF16), part.astype(BF16), preferred_element_type=F32)
         allowed = jnp.dot(part.astype(BF16), turned, preferred_element_type=F32)
         before = [jnp.zeros((1, 128), F32)]
         for i in range(16):
@@ -289,7 +307,7 @@
         rows = [jnp.sum(block, axis=0, keepdims=True)]
         for side in range(2):
             missing = 1.0 - jnp.sum(found[side], axis=0, keepdims=True)
-            rows.append(jnp.sum(picked[side], axis=0, keepdims=True) + (16.0 + side) * missing)
+            rows.append(jnp.sum(picked[side], axis=0, keepdims=True) + (8.0 + side) * missing)
         rows.append(jnp.broadcast_to(total, (1, 128)))
         rows.append(jnp.zeros((4, 128), F32))
         lists_ref[...] = jnp.concatenate(rows, axis=0).astype(jnp.int32)
@@ -309,11 +327,6 @@
         k = run * 20 + index
         arrive(unit(*node(run, a, b), run * 8 + low, count), g_send.at[k], g_recv.at[k])
 
-    def to_sibling(run, u, v, a, b):
-        k = run * 16 + u * 4 + v
-        ref = unit(*node(run, a, b), run * 8, 8)
-        push(ref, ref, s_send.at[k], s_recv.at[k], place(x, y, 1 - core))
-
     def across(run, u, a, b):
         shipment(run, 4 + 4 * u, a, b, 0, 8, first[run], ring(b + 1, 4))
         shipment(run, 5 + 4 * u, a, b, 0, 8, first[run], ring(b - 1, 4))
@@ -321,17 +334,11 @@
     for run in range(2):
         a, b = first[run], second[run]
         if run == 1:
-            project(0)
+            project(core, 0)
             far_bias()
         shipment(run, 0, a, b, 0, 8, ring(a + 1, 4), b)
         shipment(run, 1, a, b, 0, 8, ring(a - 1, 4), b)
         across(run, 0, a, b)
-        to_sibling(run, 0, 0, a, b)
-        if run == 0:
-            col_push(2)
-            col_push(6)
-    for step in (3, 5, 4):
-        col_push(step)
     for run in range(2):
         a, b = first[run], second[run]
         receive(run, 0, ring(a - 1, 4), b, 0, 8)
@@ -341,49 +348,48 @@
     for run in range(2):
         a, b = first[run], second[run]
         across(run, 1, ring(a - 1, 4), b)
-        to_sibling(run, 1, 0, ring(a - 1, 4), b)
         across(run, 2, ring(a + 1, 4), b)
-        to_sibling(run, 2, 0, ring(a + 1, 4), b)
     for run in range(2):
         a, b = first[run], second[run]
         receive(run, 2, ring(a + 2, 4), b, 0, 4)
         receive(run, 3, ring(a + 2, 4), b, 4, 4)
         across(run, 3, ring(a + 2, 4), b)
-        to_sibling(run, 3, 0, ring(a + 2, 4), b)
     take(1)
     take(-1)
+    take_shared(0)
     for u in range(4):
         for run in range(2):
             a, b = ring(first[run] + (0, -1, 1, 2)[u], 4), second[run]
             receive(run, 4 + 4 * u, a, ring(b - 1, 4), 0, 8)
             shipment(run, 6 + 4 * u, a, ring(b - 1, 4), 0, 4, first[run], ring(b + 1, 4))
-            to_sibling(run, u, 1, a, ring(b - 1, 4))
             receive(run, 5 + 4 * u, a, ring(b + 1, 4), 0, 8)
             shipment(run, 7 + 4 * u, a, ring(b + 1, 4), 4, 4, first[run], ring(b - 1, 4))
-            to_sibling(run, u, 2, a, ring(b + 1, 4))
         if u == 1:
             make_lists()
+            take_shared(1)
+        if u == 2:
+            take_shared(-1)
+            take(2)
         if u == 3:
-            take(2)
             take(-2)
+            take(3)
+            take(-3)
+            take_shared(2)
     for u in range(4):
         for run in range(2):
             a, b = ring(first[run] + (0, -1, 1, 2)[u], 4), second[run]
             receive(run, 6 + 4 * u, a, ring(b + 2, 4), 0, 4)
             receive(run, 7 + 4 * u, a, ring(b + 2, 4), 4, 4)
-            to_sibling(run, u, 3, a, ring(b + 2, 4))
-        if u >= 2:
-            take((3, -3)[u - 2])
-    take(4)
+        if u == 0:
+            take(4)
+        if u == 1:
+            take_shared(-2)
+        if u == 2:
+            take_shared(3)
+    take_shared(-3)
+    take_shared(4)
     bound_ref[0:8, :] = tops[...]
     bound_ref[8:24, :] = jnp.broadcast_to(jnp.sum(weighted * weighted, axis=1, keepdims=True), (16, 128))
-    for run in range(2):
-        for u in range(4):
-            for v in range(4):
-                a = ring(first[run] + (0, -1, 1, 2)[u], 4)
-                b = ring(second[run] + (0, -1, 1, 2)[v], 4)
-                k = run * 16 + u * 4 + v
-                arrive(unit(*node(run, a, b), run * 8, 8, 1 - core), s_send.at[k], s_recv.at[k])
     for copy in sent:
         copy.wait_send()
 
@@ -393,10 +399,10 @@
     return pl.pallas_call(
         spread_kernel,
         out_shape=(
-            jax.ShapeDtypeStruct((2, 4, 1024, 128), BF16),
-            jax.ShapeDtypeStruct((4, 16, 128, 256), BF16),
-            jax.ShapeDtypeStruct((4, 16, 256, 128), BF16),
-            jax.ShapeDtypeStruct((2, 2, 4, 2, 2, 8, 32, 256), BF16),
+            jax.ShapeDtypeStruct((2, 8, 512, 128), BF16),
+            jax.ShapeDtypeStruct((8, 16, 128, 256), BF16),
+            jax.ShapeDtypeStruct((8, 16, 256, 128), BF16),
+            jax.ShapeDtypeStruct((2, 2, 4, 2, 8, 32, 256), BF16),
             jax.ShapeDtypeStruct((24, 128), F32),
             jax.ShapeDtypeStruct((128, 128), BF16),
             jax.ShapeDtypeStruct((8, 128), jnp.int32),
@@ -412,28 +418,26 @@
             VMEM((16, 16), jnp.int32),
             VMEM((4096, 128), F32),
             VMEM((8, 4, 128, 128), BF16),
-            VMEM((4, 1024, 128), BF16),
+            VMEM((2, 4, 1024, 128), BF16),
             VMEM((2, 272, 128), BF16),
             VMEM((512, 128), BF16),
             VMEM((256, 128), F32),
             VMEM((2, 32, 256), BF16),
             VMEM((8, 128), F32),
             DMA((10,)), DMA((8,)), DMA((8,)), DMA((8,)), DMA((8,)), DMA, DMA,
-            DMA((40,)), DMA((40,)), DMA((32,)), DMA((32,)), DMA((2,)),
+            DMA((40,)), DMA((40,)), DMA((8,)), DMA((8,)), DMA((2,)),
         ],
         compiler_params=pltpu.CompilerParams(
-            collective_id=0, has_side_effects=True, vmem_limit_bytes=32 * 1024 * 1024
+            collective_id=0, has_side_effects=True, vmem_limit_bytes=20 * 1024 * 1024
         ),
         name="spread",
     )(*operands)
 
 
 def attend_kernel(
-    lists_ref, qg_ref, kbd, vbd, bias, bound_ref,
-    acc0, acc1, acc2, acc3,
-    peak,
+    lists_ref, qg_ref, kbd, vbd, bias, bound_ref, *accs_and_peak
 ):
-    accs = (acc0, acc1, acc2, acc3)
+    *accs, peak = accs_and_peak
     for acc in accs:
         acc[...] = jnp.zeros_like(acc)
     same = (
@@ -446,13 +450,13 @@
     safe = (reach + bias_reach) * 1.03 <= SAFE
 
     def query(j, i):
-        return qg_ref[0, j, pl.ds(pl.multiple_of(jnp.minimum(i, 15) * 64, 64), 64), :]
+        return qg_ref[0, j, pl.ds(pl.multiple_of(jnp.minimum(i, 7) * 64, 64), 64), :]
 
     def values_of(j, block):
         return jnp.concatenate([vbd[j, block], same], axis=1)
 
     def offset_of(i, block):
-        at = (lax.div(block, 8), jnp.minimum(i, 15))
+        at = (lax.div(block, 8), jnp.minimum(i, 7))
         n = lax.rem(block, 8)
         return [bias[at[0], at[1], half, n].astype(F32) for half in range(2)]
 
@@ -468,7 +472,7 @@
                 ids = (lists_ref[1, e], lists_ref[2, e])
                 offset = jnp.concatenate(offset_of(ids[0], block) + offset_of(ids[1], block), axis=0)
                 work.append((block, ids, offset))
-            for j in range(4):
+            for j in range(8):
                 for block, ids, offset in work:
                     queries = jnp.concatenate([query(j, i) for i in ids], axis=0)
                     score = jnp.dot(queries, kbd[j, block], preferred_element_type=F32)
@@ -490,7 +494,7 @@
             block = lists_ref[0, e]
             i = lists_ref[1 + lax.rem(n, 2), e]
             offset = jnp.concatenate(offset_of(i, block), axis=0)
-            for j in range(4):
+            for j in range(8):
                 score = jnp.dot(query(j, i), kbd[j, block], preferred_element_type=F32) + offset
                 old = peak[j, i]
                 tops = [
@@ -516,81 +520,111 @@
     whole = pl.BlockSpec(memory_space=VMEM)
     return pl.pallas_call(
         attend_kernel,
-        out_shape=[jax.ShapeDtypeStruct((18, 64, 256), F32)] * 4,
+        out_shape=[jax.ShapeDtypeStruct((10, 64, 256), F32)] * 8,
         in_specs=[pl.BlockSpec(memory_space=pltpu.SMEM)] + [whole] * 5,
-        out_specs=[whole] * 4,
-        scratch_shapes=[VMEM((4, 18, 64, 128), F32)],
-        compiler_params=pltpu.CompilerParams(vmem_limit_bytes=24 * 1024 * 1024),
+        out_specs=[whole] * 8,
+        scratch_shapes=[VMEM((8, 10, 64, 128), F32)],
+        compiler_params=pltpu.CompilerParams(vmem_limit_bytes=16 * 1024 * 1024),
         name="attend",
     )(lists, qg, kbd, vbd, bias, bound)
 
 
-def deliver_kernel(
-    acc0, acc1, acc2, acc3, qg_ref, mixing_ref, out_ref, update_ref, send_sem, recv_sem, own_sem
-):
+def deliver_kernel(*refs):
+    accs = refs[:8]
+    qg_ref, mixing_ref, out_ref, update_ref, landed, send_sem, recv_sem, own_sem = refs[8:]
     row = lax.axis_index("row")
     col = lax.axis_index("col")
     head = lax.axis_index("head")
-
-    def other(flip):
-        return (1 - head) if flip else head
-
-    def device(step, flip):
-        return (ring(row + step, 8), col, other(flip))
-
-    moves = [(step, flip) for step in (4, 3, 5, 2, 6, 1, 7) for flip in (1, 0)] + [(0, 1)]
+    core = lax.rem(col, 2)
+
+    def device(step, flip, cross):
+        return (
+            ring(row + step, 8),
+            col + 1 - 2 * core if cross else col,
+            (1 - head) if flip else head,
+        )
+
+    def from_(step, flip, cross):
+        there = device(step, flip, cross)
+        return landed.at[(1 - core) if cross else core, there[2] * 8 + there[0]]
+
+    def part(step, flip, cross):
+        there = device(step, flip, cross)
+        return update_ref.at[there[2], there[0], (1 - core) if cross else core]
+
+    steps = (4, 3, 5, 2, 6, 1, 7, 0)
+    kinds = ((1, 0), (1, 1), (0, 0), (0, 1))
+    moves = [(step, flip, cross) for step in steps for flip, cross in kinds if step or flip or cross]
     barrier = pltpu.get_barrier_semaphore()
-    for step, flip in moves:
-        pl.semaphore_signal(barrier, inc=1, device_id=device(step, flip), device_id_type=MESH)
-
-    def spot(step, flip):
-        return out_ref.at[pl.ds((other(flip) * 8 + ring(row + step, 8)) * 4, 4)]
-
-    def part(step, flip):
-        return update_ref.at[other(flip), ring(row + step, 8)]
+    for move in moves:
+        pl.semaphore_signal(barrier, inc=1, device_id=device(*move), device_id_type=MESH)
 
     def finish(step):
         target = ring(row + step, 8)
-        rows = pl.ds(pl.multiple_of(target * 128, 128), 128)
-        for j, acc in enumerate((acc0, acc1, acc2, acc3)):
-            sums = acc[pl.ds(target * 2, 2)].reshape(128, 256)
-            attention = sums[:, :128] / sums[:, 128:]
-            gated = (attention * qg_ref[1, j, rows, :].astype(F32)).astype(BF16)
-            update = lax.dot_general(mixing_ref[...], gated, NT, preferred_element_type=F32).astype(BF16)
-            update_ref[0, target, j] = update[:64, :]
-            update_ref[1, target, j] = update[64:, :]
+        rows = pl.ds(pl.multiple_of(target * 64, 64), 64)
+        for core_ in range(2):
+            for pair in range(2):
+                gated = []
+                for m in (core_ * 4 + 2 * pair, core_ * 4 + 2 * pair + 1):
+                    sums = accs[m][target]
+                    attention = sums[:, :128] / sums[:, 128:]
+                    gated.append((attention * qg_ref[1, m, rows, :].astype(F32)).astype(BF16))
+                gated = jnp.concatenate(gated, axis=0)
+                update = lax.dot_general(mixing_ref[...], gated, NT, preferred_element_type=F32).astype(BF16)
+                update_ref[0, target, core_, pair] = update[:64, :]
+                update_ref[1, target, core_, pair] = update[64:, :]
 
     copies = []
 
-    def push(step, flip):
-        k = flip * 8 + step
+    def push(step, flip, cross):
+        k = (flip * 2 + cross) * 8 + step
         copy = pltpu.make_async_remote_copy(
-            src_ref=part(step, flip), dst_ref=spot(0, 0),
+            src_ref=part(step, flip, cross), dst_ref=from_(0, 0, 0),
             send_sem=send_sem.at[k], recv_sem=recv_sem.at[k],
-            device_id=device(step, flip), device_id_type=MESH,
+            device_id=device(step, flip, cross), device_id_type=MESH,
         )
         copy.start()
         copies.append(copy)
 
+    def arrive(step, flip, cross):
+        k = (flip * 2 + cross) * 8 + step
+        ref = from_(-step, flip, cross)
+        pltpu.make_async_remote_copy(
+            src_ref=ref, dst_ref=ref, send_sem=send_sem.at[k], recv_sem=recv_sem.at[k],
+            device_id=device(0, 0, 1), device_id_type=MESH,
+        ).wait_recv()
+
     for step in (4, 3, 5):
         finish(step)
     pl.semaphore_wait(barrier, len(moves))
-    for step in (4, 3, 5, 2, 6, 1, 7, 0):
+    for step in steps:
         if step not in (4, 3, 5):
             finish(step)
-        push(step, 1)
-        if step > 0:
-            push(step, 0)
-    own = pltpu.make_async_copy(part(0, 0), spot(0, 0), own_sem)
+        for flip, cross in kinds:
+            if step or flip or cross:
+                push(step, flip, cross)
+    own = pltpu.make_async_copy(part(0, 0, 0), from_(0, 0, 0), own_sem)
     own.start()
+
+    def join(step, flip):
+        source = ((1 - head) if flip else head) * 8 + ring(row - step, 8)
+        for pair in range(2):
+            low = landed[0, source, pair]
+            high = landed[1, source, pair]
+            out_ref[source * 4 + pair * 2] = jnp.concatenate([low[:, :64], high[:, :64]], axis=1)
+            out_ref[source * 4 + pair * 2 + 1] = jnp.concatenate([low[:, 64:], high[:, 64:]], axis=1)
+
     own.wait()
-    for step, flip in moves:
-        k = flip * 8 + step
-        pltpu.make_async_remote_copy(
-            src_ref=spot(-step, flip), dst_ref=spot(-step, flip),
-            send_sem=send_sem.at[k], recv_sem=recv_sem.at[k],
-            device_id=device(step, flip), device_id_type=MESH,
-        ).wait_recv()
+    arrive(0, 0, 1)
+    join(0, 0)
+    arrive(0, 1, 0)
+    arrive(0, 1, 1)
+    join(0, 1)
+    for step in (1, 7, 2, 6, 3, 5, 4):
+        for flip in range(2):
+            arrive(step, flip, 0)
+            arrive(step, flip, 1)
+            join(step, flip)
     for copy in copies:
         copy.wait_send()
 
@@ -600,9 +634,13 @@
     return pl.pallas_call(
         deliver_kernel,
         out_shape=jax.ShapeDtypeStruct((64, 64, 128), BF16),
-        in_specs=[whole] * 6,
+        in_specs=[whole] * 10,
         out_specs=whole,
-        scratch_shapes=[VMEM((2, 8, 4, 64, 128), BF16), DMA((16,)), DMA((16,)), DMA],
+        scratch_shapes=[
+            VMEM((2, 8, 2, 2, 64, 128), BF16),
+            VMEM((2, 16, 2, 64, 128), BF16),
+            DMA((32,)), DMA((32,)), DMA,
+        ],
         compiler_params=pltpu.CompilerParams(
             collective_id=1, has_side_effects=True, vmem_limit_bytes=16 * 1024 * 1024
         ),
@@ -619,7 +657,7 @@
     qg, kbd, vbd, bias, bound, mixing, lists = spread(
         *[pltpu.with_memory_space_constraint(operand, pltpu.HBM) for operand in operands]
     )
-    accs = attend(lists, qg, kbd, vbd, bias.reshape(2, 16, 2, 8, 32, 256), bound)
+    accs = attend(lists, qg, kbd, vbd, bias.reshape(2, 8, 2, 8, 32, 256), bound)
     return jnp.transpose(deliver(accs, qg, mixing), (2, 0, 1))
 
 

time: 164 us -> 163 us (level)
    pallas_call x2, Pallas kernels: 133 us -> 130 us  [the longest x1 82.1 us: attend(): pl.pallas_call(attend_kernel, out_shape=[jax.ShapeDtypeStruct((10, 64, 25...]
    pallas_call x1, Pallas kernels: 29.8 us -> 31.7 us  [deliver(): pl.pallas_call(deliver_kernel, out_shape=jax.ShapeDtypeStruct((64, 64, 12...]
where the time goes in v5:
time: 163 us
  Pallas kernels  162 us (99%)
    pallas_call x1, Pallas kernels, attend(): pl.pallas_call(attend_kernel, out_shape=[jax.ShapeDtypeStruct((10, 64, 25...  82.1 us
    pallas_call x1, Pallas kernels, spread(): pl.pallas_call(spread_kernel, out_shape=(jax.ShapeDtypeStruct((2, 8, 512,...  48.3 us
    pallas_call x1, Pallas kernels, deliver(): pl.pallas_call(deliver_kernel, out_shape=jax.ShapeDtypeStruct((64, 64, 12...  31.7 us

profile of v5, /device:TPU:1, one launch (start us, length us, event | category | flops | bytes accessed | tf_op | source)
XLA Modules:
  0.0 163.1 jit_solution(4233881449336185761)
XLA Ops:
  0.0 48.3 %spread.1 = (bf16[2,8,512,128]{3,2,1,0:T(8,128)(2,1)S(1)}, bf16[8,16,128,256]{3,2,1,0:T(8,128)(2,1)S(1)}, bf16[8,16,256,128]{3,2,1,0:T(8,128)(2,1)S(1)}, bf16[2,...) custom-call(bf16[128,64,128]{2,1,0:T(8,128)(2,1)} %tile_ref.1, ...), custom_call_target="tpu_custom_call" | custom-call | tf_op jit(solution)/shard_map/spread/pallas_call | solution.py:399
  48.3 82.1 %attend.1 = (f32[10,64,256]{2,1,0:T(8,128)S(1)}, f32[10,64,256]{2,1,0:T(8,128)S(1)}, f32[10,64,256]{2,1,0:T(8,128)S(1)}, f32[10,64,256]{2,1,0:T(8,128)S(1)}, f32...) custom-call(s32[8,128]{1,0:T(8,128)S(1)} %get-tuple-element.20.lists, ...), custom_call_target="tpu_custom_call" | custom-call | tf_op jit(solution)/shard_map/attend/pallas_call | solution.py:521
  130.4 31.7 %deliver.1 = bf16[64,64,128]{2,1,0:T(8,128)(2,1)S(1)} custom-call(f32[10,64,256]{2,1,0:T(8,128)S(1)} %get-tuple-element.26.refs_0_, f32[10,64,256]{2,1,0:T(8,128)S(1)} %get-tuple-element.27.refs_1_, f32[10,64,256]{2,1,0:T(8,128)S(1)} %get-tuple-element.28.refs_2_, f32[10,64,256]{2,1,0:T(8,128)S(1)} %get-tuple-element.29.refs_3_, ...), custom_call_target="tpu_custom_call" | custom-call | tf_op jit(solution)/shard_map/deliver/pallas_call | solution.py:634
  162.1 1.0 copy.12

commit v6 on v4

--- a/solution.py
+++ b/solution.py
@@ -229,26 +229,11 @@
             tops[1:2, :] = jnp.maximum(tops[1:2, :], jnp.max(lengths, axis=0, keepdims=True))
             return carry
 
-        lax.fori_loop(0, 4, one, 0, unroll=2)
+        lax.fori_loop(0, 4, one, 0, unroll=True)
 
     def take(step):
         arrive(strip_rows(step), col_send.at[(8 - step) % 8], col_recv.at[(8 - step) % 8])
         project(step)
-
-    own.wait()
-    own_cols.wait()
-    for k, step in enumerate((-2, 2, -1, 1)):
-        z_arrive(k, chunk(step))
-    z_push(4, chunk(-2), chunk(-3), 1)
-    z_push(5, chunk(2), chunk(3), -1)
-    z_push(6, chunk(-2, 0, 1), chunk(4, 0, 1), 2)
-    z_push(7, chunk(2, 1, 1), chunk(4, 1, 1), -2)
-
-    def far_bias():
-        z_arrive(4, chunk(-3))
-        z_arrive(5, chunk(3))
-        z_arrive(6, chunk(4, 0, 1))
-        z_arrive(7, chunk(4, 1, 1))
 
     def make_lists():
         mixing_ref[...] = w_out_ref[...].astype(F32).T.astype(BF16)
@@ -294,6 +279,23 @@
         rows.append(jnp.zeros((4, 128), F32))
         lists_ref[...] = jnp.concatenate(rows, axis=0).astype(jnp.int32)
 
+    own_cols.wait()
+    project(0)
+    make_lists()
+    own.wait()
+    for k, step in enumerate((-2, 2, -1, 1)):
+        z_arrive(k, chunk(step))
+    z_push(4, chunk(-2), chunk(-3), 1)
+    z_push(5, chunk(2), chunk(3), -1)
+    z_push(6, chunk(-2, 0, 1), chunk(4, 0, 1), 2)
+    z_push(7, chunk(2, 1, 1), chunk(4, 1, 1), -2)
+
+    def far_bias():
+        z_arrive(4, chunk(-3))
+        z_arrive(5, chunk(3))
+        z_arrive(6, chunk(4, 0, 1))
+        z_arrive(7, chunk(4, 1, 1))
+
     def node(run, a, b):
         return (a, b) if run == 0 else (b, a)
 
@@ -321,7 +323,8 @@
     for run in range(2):
         a, b = first[run], second[run]
         if run == 1:
-            project(0)
+            take(1)
+            take(-1)
             far_bias()
         shipment(run, 0, a, b, 0, 8, ring(a + 1, 4), b)
         shipment(run, 1, a, b, 0, 8, ring(a - 1, 4), b)
@@ -350,8 +353,7 @@
         receive(run, 3, ring(a + 2, 4), b, 4, 4)
         across(run, 3, ring(a + 2, 4), b)
         to_sibling(run, 3, 0, ring(a + 2, 4), b)
-    take(1)
-    take(-1)
+    take(2)
     for u in range(4):
         for run in range(2):
             a, b = ring(first[run] + (0, -1, 1, 2)[u], 4), second[run]
@@ -362,18 +364,17 @@
             shipment(run, 7 + 4 * u, a, ring(b + 1, 4), 4, 4, first[run], ring(b - 1, 4))
             to_sibling(run, u, 2, a, ring(b + 1, 4))
         if u == 1:
-            make_lists()
+            take(-2)
         if u == 3:
-            take(2)
-            take(-2)
+            take(3)
     for u in range(4):
         for run in range(2):
             a, b = ring(first[run] + (0, -1, 1, 2)[u], 4), second[run]
             receive(run, 6 + 4 * u, a, ring(b + 2, 4), 0, 4)
             receive(run, 7 + 4 * u, a, ring(b + 2, 4), 4, 4)
             to_sibling(run, u, 3, a, ring(b + 2, 4))
-        if u >= 2:
-            take((3, -3)[u - 2])
+        if u == 3:
+            take(-3)
     take(4)
     bound_ref[0:8, :] = tops[...]
     bound_ref[8:24, :] = jnp.broadcast_to(jnp.sum(weighted * weighted, axis=1, keepdims=True), (16, 128))
@@ -429,9 +430,9 @@
 
 
 def attend_kernel(
-    lists_ref, qg_ref, kbd, vbd, bias, bound_ref,
-    acc0, acc1, acc2, acc3,
-    peak,
+    lists_ref, qg_ref, kbd, vbd, bias, bound_ref, mixing_ref,
+    update_ref,
+    acc0, acc1, acc2, acc3, peak,
 ):
     accs = (acc0, acc1, acc2, acc3)
     for acc in accs:
@@ -511,58 +512,60 @@
 
         lax.fori_loop(0, 2 * total_pairs, step, 0)
 
-
-def attend(lists, qg, kbd, vbd, bias, bound):
-    whole = pl.BlockSpec(memory_space=VMEM)
-    return pl.pallas_call(
-        attend_kernel,
-        out_shape=[jax.ShapeDtypeStruct((18, 64, 256), F32)] * 4,
-        in_specs=[pl.BlockSpec(memory_space=pltpu.SMEM)] + [whole] * 5,
-        out_specs=[whole] * 4,
-        scratch_shapes=[VMEM((4, 18, 64, 128), F32)],
-        compiler_params=pltpu.CompilerParams(vmem_limit_bytes=24 * 1024 * 1024),
-        name="attend",
-    )(lists, qg, kbd, vbd, bias, bound)
-
-
-def deliver_kernel(
-    acc0, acc1, acc2, acc3, qg_ref, mixing_ref, out_ref, update_ref, send_sem, recv_sem, own_sem
-):
-    row = lax.axis_index("row")
-    col = lax.axis_index("col")
-    head = lax.axis_index("head")
-
-    def other(flip):
-        return (1 - head) if flip else head
-
-    def device(step, flip):
-        return (ring(row + step, 8), col, other(flip))
-
-    moves = [(step, flip) for step in (4, 3, 5, 2, 6, 1, 7) for flip in (1, 0)] + [(0, 1)]
-    barrier = pltpu.get_barrier_semaphore()
-    for step, flip in moves:
-        pl.semaphore_signal(barrier, inc=1, device_id=device(step, flip), device_id_type=MESH)
-
-    def spot(step, flip):
-        return out_ref.at[pl.ds((other(flip) * 8 + ring(row + step, 8)) * 4, 4)]
-
-    def part(step, flip):
-        return update_ref.at[other(flip), ring(row + step, 8)]
-
-    def finish(step):
-        target = ring(row + step, 8)
+    def finish(target, carry):
         rows = pl.ds(pl.multiple_of(target * 128, 128), 128)
-        for j, acc in enumerate((acc0, acc1, acc2, acc3)):
-            sums = acc[pl.ds(target * 2, 2)].reshape(128, 256)
+        for j in range(4):
+            sums = accs[j][pl.ds(target * 2, 2)].reshape(128, 256)
             attention = sums[:, :128] / sums[:, 128:]
             gated = (attention * qg_ref[1, j, rows, :].astype(F32)).astype(BF16)
             update = lax.dot_general(mixing_ref[...], gated, NT, preferred_element_type=F32).astype(BF16)
             update_ref[0, target, j] = update[:64, :]
             update_ref[1, target, j] = update[64:, :]
-
+        return carry
+
+    lax.fori_loop(0, 8, finish, 0, unroll=2)
+
+
+def attend(lists, qg, kbd, vbd, bias, bound, mixing):
+    whole = pl.BlockSpec(memory_space=VMEM)
+    return pl.pallas_call(
+        attend_kernel,
+        out_shape=jax.ShapeDtypeStruct((2, 8, 4, 64, 128), BF16),
+        in_specs=[pl.BlockSpec(memory_space=pltpu.SMEM)] + [whole] * 6,
+        out_specs=whole,
+        scratch_shapes=[VMEM((18, 64, 256), F32)] * 4 + [VMEM((4, 18, 64, 128), F32)],
+        compiler_params=pltpu.CompilerParams(vmem_limit_bytes=24 * 1024 * 1024),
+        name="attend",
+    )(lists, qg, kbd, vbd, bias, bound, mixing)
+
+
+def deliver_kernel(update_ref, out_ref, send_sem, recv_sem, own_sem):
+    row = lax.axis_index("row")
+    col = lax.axis_index("col")
+    head = lax.axis_index("head")
+
+    def other(flip):
+        return (1 - head) if flip else head
+
+    def device(step, flip):
+        return (ring(row + step, 8), col, other(flip))
+
+    moves = [(step, flip) for step in (4, 3, 5, 2, 6, 1, 7) for flip in (1, 0)] + [(0, 1)]
+    barrier = pltpu.get_barrier_semaphore()
+    for step, flip in moves:
+        pl.semaphore_signal(barrier, inc=1, device_id=device(step, flip), device_id_type=MESH)
+
+    def spot(step, flip):
+        return out_ref.at[pl.ds((other(flip) * 8 + ring(row + step, 8)) * 4, 4)]
+
+    def part(step, flip):
+        return update_ref.at[other(flip), ring(row + step, 8)]
+
+    own = pltpu.make_async_copy(part(0, 0), spot(0, 0), own_sem)
+    own.start()
+    pl.semaphore_wait(barrier, len(moves))
     copies = []
-
-    def push(step, flip):
+    for step, flip in moves:
         k = flip * 8 + step
         copy = pltpu.make_async_remote_copy(
             src_ref=part(step, flip), dst_ref=spot(0, 0),
@@ -571,18 +574,6 @@
         )
         copy.start()
         copies.append(copy)
-
-    for step in (4, 3, 5):
-        finish(step)
-    pl.semaphore_wait(barrier, len(moves))
-    for step in (4, 3, 5, 2, 6, 1, 7, 0):
-        if step not in (4, 3, 5):
-            finish(step)
-        push(step, 1)
-        if step > 0:
-            push(step, 0)
-    own = pltpu.make_async_copy(part(0, 0), spot(0, 0), own_sem)
-    own.start()
     own.wait()
     for step, flip in moves:
         k = flip * 8 + step
@@ -595,19 +586,19 @@
         copy.wait_send()
 
 
-def deliver(accs, qg, mixing):
+def deliver(update):
     whole = pl.BlockSpec(memory_space=VMEM)
     return pl.pallas_call(
         deliver_kernel,
         out_shape=jax.ShapeDtypeStruct((64, 64, 128), BF16),
-        in_specs=[whole] * 6,
+        in_specs=[whole],
         out_specs=whole,
-        scratch_shapes=[VMEM((2, 8, 4, 64, 128), BF16), DMA((16,)), DMA((16,)), DMA],
+        scratch_shapes=[DMA((16,)), DMA((16,)), DMA],
         compiler_params=pltpu.CompilerParams(
             collective_id=1, has_side_effects=True, vmem_limit_bytes=16 * 1024 * 1024
         ),
         name="deliver",
-    )(*accs, qg, mixing)
+    )(update)
 
 
 def per_device(
@@ -619,8 +610,8 @@
     qg, kbd, vbd, bias, bound, mixing, lists = spread(
         *[pltpu.with_memory_space_constraint(operand, pltpu.HBM) for operand in operands]
     )
-    accs = attend(lists, qg, kbd, vbd, bias.reshape(2, 16, 2, 8, 32, 256), bound)
-    return jnp.transpose(deliver(accs, qg, mixing), (2, 0, 1))
+    update = attend(lists, qg, kbd, vbd, bias.reshape(2, 16, 2, 8, 32, 256), bound, mixing)
+    return jnp.transpose(deliver(update), (2, 0, 1))
 
 
 def solution(mesh):

time: 164 us -> 152 us (0.927)
  Pallas kernels: 163 us -> 151 us
    pallas_call x1, Pallas kernels: 85.5 us -> 74 us  [attend(): pl.pallas_call(attend_kernel, out_shape=jax.ShapeDtypeStruct((2, 8, 4, 64...]
where the time goes in v6:
time: 152 us
  Pallas kernels  151 us (99%)
    pallas_call x1, Pallas kernels, attend(): pl.pallas_call(attend_kernel, out_shape=jax.ShapeDtypeStruct((2, 8, 4, 64...  74 us
    pallas_call x1, Pallas kernels, spread(): pl.pallas_call(spread_kernel, out_shape=(jax.ShapeDtypeStruct((2, 4, 1024...  47.5 us
    pallas_call x1, Pallas kernels, deliver(): pl.pallas_call(deliver_kernel, out_shape=jax.ShapeDtypeStruct((64, 64, 12...  29.8 us

profile of v6, /device:TPU:1, one launch (start us, length us, event | category | flops | bytes accessed | tf_op | source)
XLA Modules:
  0.0 152.2 jit_solution(15135243385234132447)
XLA Ops:
  0.0 47.5 %spread.1 = (bf16[2,4,1024,128]{3,2,1,0:T(8,128)(2,1)S(1)}, bf16[4,16,128,256]{3,2,1,0:T(8,128)(2,1)S(1)}, bf16[4,16,256,128]{3,2,1,0:T(8,128)(2,1)S(1)}, bf16[2...) custom-call(bf16[128,64,128]{2,1,0:T(8,128)(2,1)} %tile_ref.1, ...), custom_call_target="tpu_custom_call" | custom-call | tf_op jit(solution)/shard_map/spread/pallas_call | solution.py:394
  47.5 74.0 %attend.1.update_ref = bf16[2,8,4,64,128]{4,3,2,1,0:T(8,128)(2,1)S(1)} custom-call(s32[8,128]{1,0:T(8,128)S(1)} %get-tuple-element.12.lists_ref, bf16[2,4,1024,128]{3,2,1,0:T(8,128)(2,1)S(1)} %get-tuple-element.13.qg_ref, bf16[4,16,128,256]{3,2,1,0:T(8,128)(2,1)S(1)} %get-tuple-element.14.kbd, bf16[4,16,256,128]{3,2,1,0:T(8,128)(2,1)S(1)} %get-tuple-element.15.vbd, ...), custom_call_target="tpu_custom_call" | custom-call | tf_op jit(solution)/shard_map/attend/pallas_call | solution.py:531
  121.4 29.8 %deliver.1 = bf16[64,64,128]{2,1,0:T(8,128)(2,1)S(1)} custom-call(bf16[2,8,4,64,128]{4,3,2,1,0:T(8,128)(2,1)S(1)} %attend.1.update_ref), custom_call_target="tpu_custom_call" | custom-call | tf_op jit(solution)/shard_map/deliver/pallas_call | solution.py:591
  151.2 1.0 copy.12

commit v7 on v4

--- a/solution.py
+++ b/solution.py
@@ -155,9 +155,9 @@
     bsend[0] = jnp.concatenate([b[:, :64] for b in by_head], axis=1).astype(BF16)
     bsend[1] = jnp.concatenate([b[:, 64:] for b in by_head], axis=1).astype(BF16)
 
-    def unit(x_, y_, low, count, core_=None):
+    def unit(x_, y_, run, low, count, core_=None):
         return bias_ref.at[
-            low // 8, lax.rem(y_, 2), x_, core if core_ is None else core_, lax.div(y_, 2), pl.ds(low % 8, count)
+            run, lax.rem(y_, 2), x_, core if core_ is None else core_, lax.div(y_, 2), pl.ds(low, count)
         ]
 
     def arrive(dst, send_sem, recv_sem):
@@ -169,8 +169,10 @@
     def slot(step):
         return 2 * step - 1 if step > 0 else -2 * step
 
+    spans = ((0, 2, 5), (5, 7, 8))
+
     def chunk(step, low=0, count=2):
-        return unit(x, y, 2 * slot(step) + low, count)
+        return bias_ref.at[pl.ds(low, count), lax.rem(y, 2), x, core, lax.div(y, 2), slot(step)]
 
     def z_push(k, src, dst, step):
         push(src, dst, z_send.at[k], z_recv.at[k], along_z(step))
@@ -229,26 +231,11 @@
             tops[1:2, :] = jnp.maximum(tops[1:2, :], jnp.max(lengths, axis=0, keepdims=True))
             return carry
 
-        lax.fori_loop(0, 4, one, 0, unroll=2)
+        lax.fori_loop(0, 4, one, 0, unroll=True)
 
     def take(step):
         arrive(strip_rows(step), col_send.at[(8 - step) % 8], col_recv.at[(8 - step) % 8])
         project(step)
-
-    own.wait()
-    own_cols.wait()
-    for k, step in enumerate((-2, 2, -1, 1)):
-        z_arrive(k, chunk(step))
-    z_push(4, chunk(-2), chunk(-3), 1)
-    z_push(5, chunk(2), chunk(3), -1)
-    z_push(6, chunk(-2, 0, 1), chunk(4, 0, 1), 2)
-    z_push(7, chunk(2, 1, 1), chunk(4, 1, 1), -2)
-
-    def far_bias():
-        z_arrive(4, chunk(-3))
-        z_arrive(5, chunk(3))
-        z_arrive(6, chunk(4, 0, 1))
-        z_arrive(7, chunk(4, 1, 1))
 
     def make_lists():
         mixing_ref[...] = w_out_ref[...].astype(F32).T.astype(BF16)
@@ -294,86 +281,137 @@
         rows.append(jnp.zeros((4, 128), F32))
         lists_ref[...] = jnp.concatenate(rows, axis=0).astype(jnp.int32)
 
+    own_cols.wait()
+    project(0)
+    make_lists()
+    own.wait()
+    for k, step in enumerate((-2, 2, -1, 1)):
+        z_arrive(k, chunk(step))
+    z_push(4, chunk(-2), chunk(-3), 1)
+    z_push(5, chunk(2), chunk(3), -1)
+    z_push(6, chunk(-2, 0, 1), chunk(4, 0, 1), 2)
+    z_push(7, chunk(2, 1, 1), chunk(4, 1, 1), -2)
+
+    def far_bias():
+        z_arrive(4, chunk(-3))
+        z_arrive(5, chunk(3))
+        z_arrive(6, chunk(4, 0, 1))
+        z_arrive(7, chunk(4, 1, 1))
+
     def node(run, a, b):
         return (a, b) if run == 0 else (b, a)
 
     first = (x, y)
     second = (y, x)
 
-    def shipment(run, index, a, b, low, count, to_a, to_b):
-        k = run * 20 + index
-        ref = unit(*node(run, a, b), run * 8 + low, count)
+    def whole_of(span):
+        return span[0], span[2] - span[0]
+
+    def halves_of(span):
+        return (span[0], span[1] - span[0]), (span[1], span[2] - span[1])
+
+    def shipment(far, run, index, a, b, rows, to_a, to_b):
+        k = far * 40 + run * 20 + index
+        ref = unit(*node(run, a, b), run, *rows)
         push(ref, ref, g_send.at[k], g_recv.at[k], place(*node(run, to_a, to_b)))
 
-    def receive(run, index, a, b, low, count):
-        k = run * 20 + index
-        arrive(unit(*node(run, a, b), run * 8 + low, count), g_send.at[k], g_recv.at[k])
-
-    def to_sibling(run, u, v, a, b):
+    def receive(far, run, index, a, b, rows):
+        k = far * 40 + run * 20 + index
+        arrive(unit(*node(run, a, b), run, *rows), g_send.at[k], g_recv.at[k])
+
+    def to_sibling(run, u, v):
         k = run * 16 + u * 4 + v
-        ref = unit(*node(run, a, b), run * 8, 8)
+        a, b = ring(first[run] + (0, -1, 1, 2)[u], 4), ring(second[run] + (0, -1, 1, 2)[v], 4)
+        ref = unit(*node(run, a, b), run, 0, 8)
         push(ref, ref, s_send.at[k], s_recv.at[k], place(x, y, 1 - core))
 
-    def across(run, u, a, b):
-        shipment(run, 4 + 4 * u, a, b, 0, 8, first[run], ring(b + 1, 4))
-        shipment(run, 5 + 4 * u, a, b, 0, 8, first[run], ring(b - 1, 4))
-
-    for run in range(2):
-        a, b = first[run], second[run]
-        if run == 1:
-            project(0)
-            far_bias()
-        shipment(run, 0, a, b, 0, 8, ring(a + 1, 4), b)
-        shipment(run, 1, a, b, 0, 8, ring(a - 1, 4), b)
-        across(run, 0, a, b)
-        to_sibling(run, 0, 0, a, b)
-        if run == 0:
-            col_push(2)
-            col_push(6)
-    for step in (3, 5, 4):
+    def begin(far, run):
+        a, b, rows = first[run], second[run], whole_of(spans[far])
+        shipment(far, run, 0, a, b, rows, ring(a + 1, 4), b)
+        shipment(far, run, 1, a, b, rows, ring(a - 1, 4), b)
+
+    def across(far, run, u):
+        a, b, rows = ring(first[run] + (0, -1, 1, 2)[u], 4), second[run], whole_of(spans[far])
+        shipment(far, run, 4 + 4 * u, a, b, rows, first[run], ring(b + 1, 4))
+        shipment(far, run, 5 + 4 * u, a, b, rows, first[run], ring(b - 1, 4))
+
+    def pass_first(far, run):
+        a, b, rows = first[run], second[run], whole_of(spans[far])
+        low, high = halves_of(spans[far])
+        receive(far, run, 0, ring(a - 1, 4), b, rows)
+        shipment(far, run, 2, ring(a - 1, 4), b, low, ring(a + 1, 4), b)
+        receive(far, run, 1, ring(a + 1, 4), b, rows)
+        shipment(far, run, 3, ring(a + 1, 4), b, high, ring(a - 1, 4), b)
+
+    def end_first(far, run):
+        a, b = ring(first[run] + 2, 4), second[run]
+        low, high = halves_of(spans[far])
+        receive(far, run, 2, a, b, low)
+        receive(far, run, 3, a, b, high)
+
+    def pass_second(far, run, u):
+        a, b, rows = ring(first[run] + (0, -1, 1, 2)[u], 4), second[run], whole_of(spans[far])
+        low, high = halves_of(spans[far])
+        receive(far, run, 4 + 4 * u, a, ring(b - 1, 4), rows)
+        shipment(far, run, 6 + 4 * u, a, ring(b - 1, 4), low, first[run], ring(b + 1, 4))
+        receive(far, run, 5 + 4 * u, a, ring(b + 1, 4), rows)
+        shipment(far, run, 7 + 4 * u, a, ring(b + 1, 4), high, first[run], ring(b - 1, 4))
+
+    def end_second(far, run, u):
+        a, b = ring(first[run] + (0, -1, 1, 2)[u], 4), ring(second[run] + 2, 4)
+        low, high = halves_of(spans[far])
+        receive(far, run, 6 + 4 * u, a, b, low)
+        receive(far, run, 7 + 4 * u, a, b, high)
+
+    for run in range(2):
+        begin(0, run)
+    for run in range(2):
+        across(0, run, 0)
+    for step in (2, 6, 3, 5, 4):
         col_push(step)
-    for run in range(2):
-        a, b = first[run], second[run]
-        receive(run, 0, ring(a - 1, 4), b, 0, 8)
-        shipment(run, 2, ring(a - 1, 4), b, 0, 4, ring(a + 1, 4), b)
-        receive(run, 1, ring(a + 1, 4), b, 0, 8)
-        shipment(run, 3, ring(a + 1, 4), b, 4, 4, ring(a - 1, 4), b)
-    for run in range(2):
-        a, b = first[run], second[run]
-        across(run, 1, ring(a - 1, 4), b)
-        to_sibling(run, 1, 0, ring(a - 1, 4), b)
-        across(run, 2, ring(a + 1, 4), b)
-        to_sibling(run, 2, 0, ring(a + 1, 4), b)
-    for run in range(2):
-        a, b = first[run], second[run]
-        receive(run, 2, ring(a + 2, 4), b, 0, 4)
-        receive(run, 3, ring(a + 2, 4), b, 4, 4)
-        across(run, 3, ring(a + 2, 4), b)
-        to_sibling(run, 3, 0, ring(a + 2, 4), b)
     take(1)
     take(-1)
+    far_bias()
+    for run in range(2):
+        begin(1, run)
+    for run in range(2):
+        across(1, run, 0)
+    for run in range(2):
+        to_sibling(run, 0, 0)
+    for far in range(2):
+        for run in range(2):
+            pass_first(far, run)
+        for run in range(2):
+            across(far, run, 1)
+            across(far, run, 2)
+    for run in range(2):
+        to_sibling(run, 1, 0)
+        to_sibling(run, 2, 0)
+    for far in range(2):
+        for run in range(2):
+            end_first(far, run)
+            across(far, run, 3)
+    for run in range(2):
+        to_sibling(run, 3, 0)
+    take(2)
+    for u in range(4):
+        for far in range(2):
+            for run in range(2):
+                pass_second(far, run, u)
+        for run in range(2):
+            to_sibling(run, u, 1)
+            to_sibling(run, u, 2)
+        if u == 1:
+            take(-2)
+        if u == 3:
+            take(3)
     for u in range(4):
         for run in range(2):
-            a, b = ring(first[run] + (0, -1, 1, 2)[u], 4), second[run]
-            receive(run, 4 + 4 * u, a, ring(b - 1, 4), 0, 8)
-            shipment(run, 6 + 4 * u, a, ring(b - 1, 4), 0, 4, first[run], ring(b + 1, 4))
-            to_sibling(run, u, 1, a, ring(b - 1, 4))
-            receive(run, 5 + 4 * u, a, ring(b + 1, 4), 0, 8)
-            shipment(run, 7 + 4 * u, a, ring(b + 1, 4), 4, 4, first[run], ring(b - 1, 4))
-            to_sibling(run, u, 2, a, ring(b + 1, 4))
-        if u == 1:
-            make_lists()
-        if u == 3:
-            take(2)
-            take(-2)
-    for u in range(4):
-        for run in range(2):
-            a, b = ring(first[run] + (0, -1, 1, 2)[u], 4), second[run]
-            receive(run, 6 + 4 * u, a, ring(b + 2, 4), 0, 4)
-            receive(run, 7 + 4 * u, a, ring(b + 2, 4), 4, 4)
-            to_sibling(run, u, 3, a, ring(b + 2, 4))
-        if u >= 2:
-            take((3, -3)[u - 2])
+            for far in range(2):
+                end_second(far, run, u)
+            to_sibling(run, u, 3)
+        if u == 2:
+            take(-3)
     take(4)
     bound_ref[0:8, :] = tops[...]
     bound_ref[8:24, :] = jnp.broadcast_to(jnp.sum(weighted * weighted, axis=1, keepdims=True), (16, 128))
@@ -383,7 +421,7 @@
                 a = ring(first[run] + (0, -1, 1, 2)[u], 4)
                 b = ring(second[run] + (0, -1, 1, 2)[v], 4)
                 k = run * 16 + u * 4 + v
-                arrive(unit(*node(run, a, b), run * 8, 8, 1 - core), s_send.at[k], s_recv.at[k])
+                arrive(unit(*node(run, a, b), run, 0, 8, 1 - core), s_send.at[k], s_recv.at[k])
     for copy in sent:
         copy.wait_send()
 
@@ -419,7 +457,7 @@
             VMEM((2, 32, 256), BF16),
             VMEM((8, 128), F32),
             DMA((10,)), DMA((8,)), DMA((8,)), DMA((8,)), DMA((8,)), DMA, DMA,
-            DMA((40,)), DMA((40,)), DMA((32,)), DMA((32,)), DMA((2,)),
+            DMA((80,)), DMA((80,)), DMA((32,)), DMA((32,)), DMA((2,)),
         ],
         compiler_params=pltpu.CompilerParams(
             collective_id=0, has_side_effects=True, vmem_limit_bytes=32 * 1024 * 1024
@@ -452,8 +490,8 @@
         return jnp.concatenate([vbd[j, block], same], axis=1)
 
     def offset_of(i, block):
-        at = (lax.div(block, 8), jnp.minimum(i, 15))
-        n = lax.rem(block, 8)
+        at = (lax.rem(block, 2), jnp.minimum(i, 15))
+        n = lax.div(block, 2)
         return [bias[at[0], at[1], half, n].astype(F32) for half in range(2)]
 
     total_pairs = lists_ref[3, 0]

time: 164 us -> 171 us (1.043)
  Pallas kernels: 163 us -> 170 us
    pallas_call x1, Pallas kernels: 85.5 us -> 92.9 us  [attend(): pl.pallas_call(attend_kernel, out_shape=[jax.ShapeDtypeStruct((18, 64, 25...]
where the time goes in v7:
time: 171 us
  Pallas kernels  170 us (99%)
    pallas_call x1, Pallas kernels, attend(): pl.pallas_call(attend_kernel, out_shape=[jax.ShapeDtypeStruct((18, 64, 25...  92.9 us
    pallas_call x1, Pallas kernels, spread(): pl.pallas_call(spread_kernel, out_shape=(jax.ShapeDtypeStruct((2, 4, 1024...  47.4 us
    pallas_call x1, Pallas kernels, deliver(): pl.pallas_call(deliver_kernel, out_shape=jax.ShapeDtypeStruct((64, 64, 12...  29.7 us

profile of v7, /device:TPU:1, one launch (start us, length us, event | category | flops | bytes accessed | tf_op | source)
XLA Modules:
  0.0 170.9 jit_solution(12383464475799420943)
XLA Ops:
  0.0 47.4 %spread.1 = (bf16[2,4,1024,128]{3,2,1,0:T(8,128)(2,1)S(1)}, bf16[4,16,128,256]{3,2,1,0:T(8,128)(2,1)S(1)}, bf16[4,16,256,128]{3,2,1,0:T(8,128)(2,1)S(1)}, bf16[2...) custom-call(bf16[128,64,128]{2,1,0:T(8,128)(2,1)} %tile_ref.1, ...), custom_call_target="tpu_custom_call" | custom-call | tf_op jit(solution)/shard_map/spread/pallas_call | solution.py:431
  47.5 92.9 %attend.1 = (f32[18,64,256]{2,1,0:T(8,128)S(1)}, f32[18,64,256]{2,1,0:T(8,128)S(1)}, f32[18,64,256]{2,1,0:T(8,128)S(1)}, f32[18,64,256]{2,1,0:T(8,128)S(1)}) custom-call(s32[8,128]{1,0:T(8,128)S(1)} %get-tuple-element.16.lists_ref, bf16[2,4,1024,128]{3,2,1,0:T(8,128)(2,1)S(1)} %get-tuple-element.17.qg_ref, ...), custom_call_target="tpu_custom_call" | custom-call | tf_op jit(solution)/shard_map/attend/pallas_call | solution.py:555
  140.3 29.7 %deliver.1 = bf16[64,64,128]{2,1,0:T(8,128)(2,1)S(1)} custom-call(f32[18,64,256]{2,1,0:T(8,128)S(1)} %get-tuple-element.22.acc0, f32[18,64,256]{2,1,0:T(8,128)S(1)} %get-tuple-element.23.acc1, f32[18,64,256]{2,1,0:T(8,128)S(1)} %get-tuple-element.24.acc2, f32[18,64,256]{2,1,0:T(8,128)S(1)} %get-tuple-element.25.acc3, ...), custom_call_target="tpu_custom_call" | custom-call | tf_op jit(solution)/shard_map/deliver/pallas_call | solution.py:638
  170.0 1.0 copy.12

commit v8 on v7

--- a/solution.py
+++ b/solution.py
@@ -564,7 +564,8 @@
 
 
 def deliver_kernel(
-    acc0, acc1, acc2, acc3, qg_ref, mixing_ref, out_ref, update_ref, send_sem, recv_sem, own_sem
+    acc0, acc1, acc2, acc3, qg_ref, mixing_ref, out_ref,
+    update_ref, relay, send_sem, recv_sem, own_sem,
 ):
     row = lax.axis_index("row")
     col = lax.axis_index("col")
@@ -576,10 +577,12 @@
     def device(step, flip):
         return (ring(row + step, 8), col, other(flip))
 
-    moves = [(step, flip) for step in (4, 3, 5, 2, 6, 1, 7) for flip in (1, 0)] + [(0, 1)]
+    steps = (4, 3, 5, 2, 6, 1, 7, 0)
+    partner = device(0, 1)
+    peers = [partner] + [device(step, 0) for step in steps if step]
     barrier = pltpu.get_barrier_semaphore()
-    for step, flip in moves:
-        pl.semaphore_signal(barrier, inc=1, device_id=device(step, flip), device_id_type=MESH)
+    for peer in peers:
+        pl.semaphore_signal(barrier, inc=1, device_id=peer, device_id_type=MESH)
 
     def spot(step, flip):
         return out_ref.at[pl.ds((other(flip) * 8 + ring(row + step, 8)) * 4, 4)]
@@ -600,35 +603,42 @@
 
     copies = []
 
-    def push(step, flip):
-        k = flip * 8 + step
+    def push(k, src, dst, target):
         copy = pltpu.make_async_remote_copy(
-            src_ref=part(step, flip), dst_ref=spot(0, 0),
-            send_sem=send_sem.at[k], recv_sem=recv_sem.at[k],
-            device_id=device(step, flip), device_id_type=MESH,
+            src_ref=src, dst_ref=dst, send_sem=send_sem.at[k], recv_sem=recv_sem.at[k],
+            device_id=target, device_id_type=MESH,
         )
         copy.start()
         copies.append(copy)
 
+    def arrive(k, ref):
+        pltpu.make_async_remote_copy(
+            src_ref=ref, dst_ref=ref, send_sem=send_sem.at[k], recv_sem=recv_sem.at[k],
+            device_id=partner, device_id_type=MESH,
+        ).wait_recv()
+
     for step in (4, 3, 5):
         finish(step)
-    pl.semaphore_wait(barrier, len(moves))
-    for step in (4, 3, 5, 2, 6, 1, 7, 0):
+    pl.semaphore_wait(barrier, len(peers))
+    for step in steps:
         if step not in (4, 3, 5):
             finish(step)
-        push(step, 1)
-        if step > 0:
-            push(step, 0)
+        if step:
+            push(step, part(step, 1), relay.at[step - 1], partner)
+            push(8 + step, part(step, 0), spot(0, 0), device(step, 0))
+        else:
+            push(0, part(0, 1), spot(0, 0), partner)
     own = pltpu.make_async_copy(part(0, 0), spot(0, 0), own_sem)
     own.start()
+    for step in steps[:-1]:
+        arrive(step, relay.at[step - 1])
+        push(16 + step, relay.at[step - 1], spot(0, 1), device(step, 0))
     own.wait()
-    for step, flip in moves:
-        k = flip * 8 + step
-        pltpu.make_async_remote_copy(
-            src_ref=spot(-step, flip), dst_ref=spot(-step, flip),
-            send_sem=send_sem.at[k], recv_sem=recv_sem.at[k],
-            device_id=device(step, flip), device_id_type=MESH,
-        ).wait_recv()
+    arrive(0, spot(0, 1))
+    for step in steps[:-1]:
+        arrive(8 + step, spot(-step, 0))
+    for step in steps[:-1]:
+        arrive(16 + step, spot(-step, 1))
     for copy in copies:
         copy.wait_send()
 
@@ -640,7 +650,7 @@
         out_shape=jax.ShapeDtypeStruct((64, 64, 128), BF16),
         in_specs=[whole] * 6,
         out_specs=whole,
-        scratch_shapes=[VMEM((2, 8, 4, 64, 128), BF16), DMA((16,)), DMA((16,)), DMA],
+        scratch_shapes=[VMEM((2, 8, 4, 64, 128), BF16), VMEM((7, 4, 64, 128), BF16), DMA((24,)), DMA((24,)), DMA],
         compiler_params=pltpu.CompilerParams(
             collective_id=1, has_side_effects=True, vmem_limit_bytes=16 * 1024 * 1024
         ),

time: 171 us -> 170 us (level)
  no operation moved by 1% of the time
where the time goes in v8:
time: 170 us
  Pallas kernels  169 us (99%)
    pallas_call x1, Pallas kernels, attend(): pl.pallas_call(attend_kernel, out_shape=[jax.ShapeDtypeStruct((18, 64, 25...  92.9 us
    pallas_call x1, Pallas kernels, spread(): pl.pallas_call(spread_kernel, out_shape=(jax.ShapeDtypeStruct((2, 4, 1024...  47.4 us
    pallas_call x1, Pallas kernels, deliver(): pl.pallas_call(deliver_kernel, out_shape=jax.ShapeDtypeStruct((64, 64, 12...  28.3 us

profile of v8, /device:TPU:1, one launch (start us, length us, event | category | flops | bytes accessed | tf_op | source)
XLA Modules:
  0.0 169.6 jit_solution(17564886344137133563)
XLA Ops:
  0.0 47.4 %spread.1 = (bf16[2,4,1024,128]{3,2,1,0:T(8,128)(2,1)S(1)}, bf16[4,16,128,256]{3,2,1,0:T(8,128)(2,1)S(1)}, bf16[4,16,256,128]{3,2,1,0:T(8,128)(2,1)S(1)}, bf16[2...) custom-call(bf16[128,64,128]{2,1,0:T(8,128)(2,1)} %tile_ref.1, ...), custom_call_target="tpu_custom_call" | custom-call | tf_op jit(solution)/shard_map/spread/pallas_call | solution.py:431
  47.5 92.9 %attend.1 = (f32[18,64,256]{2,1,0:T(8,128)S(1)}, f32[18,64,256]{2,1,0:T(8,128)S(1)}, f32[18,64,256]{2,1,0:T(8,128)S(1)}, f32[18,64,256]{2,1,0:T(8,128)S(1)}) custom-call(s32[8,128]{1,0:T(8,128)S(1)} %get-tuple-element.16.lists_ref, bf16[2,4,1024,128]{3,2,1,0:T(8,128)(2,1)S(1)} %get-tuple-element.17.qg_ref, ...), custom_call_target="tpu_custom_call" | custom-call | tf_op jit(solution)/shard_map/attend/pallas_call | solution.py:555
  140.3 28.3 %deliver.1 = bf16[64,64,128]{2,1,0:T(8,128)(2,1)S(1)} custom-call(f32[18,64,256]{2,1,0:T(8,128)S(1)} %get-tuple-element.22.acc0, f32[18,64,256]{2,1,0:T(8,128)S(1)} %get-tuple-element.23.acc1, f32[18,64,256]{2,1,0:T(8,128)S(1)} %get-tuple-element.24.acc2, f32[18,64,256]{2,1,0:T(8,128)S(1)} %get-tuple-element.25.acc3, ...), custom_call_target="tpu_custom_call" | custom-call | tf_op jit(solution)/shard_map/deliver/pallas_call | solution.py:648
  168.6 1.0 copy.12

commit v9 on v8

--- a/solution.py
+++ b/solution.py
@@ -565,7 +565,7 @@
 
 def deliver_kernel(
     acc0, acc1, acc2, acc3, qg_ref, mixing_ref, out_ref,
-    update_ref, relay, send_sem, recv_sem, own_sem,
+    update_ref, relay, midway, send_sem, recv_sem, own_sem,
 ):
     row = lax.axis_index("row")
     col = lax.axis_index("col")
@@ -584,8 +584,8 @@
     for peer in peers:
         pl.semaphore_signal(barrier, inc=1, device_id=peer, device_id_type=MESH)
 
-    def spot(step, flip):
-        return out_ref.at[pl.ds((other(flip) * 8 + ring(row + step, 8)) * 4, 4)]
+    def spot(step, flip, low=0, count=4):
+        return out_ref.at[pl.ds((other(flip) * 8 + ring(row + step, 8)) * 4 + low, count)]
 
     def part(step, flip):
         return update_ref.at[other(flip), ring(row + step, 8)]
@@ -617,6 +617,19 @@
             device_id=partner, device_id_type=MESH,
         ).wait_recv()
 
+    ways = (2, -2)
+
+    def half_way(flip, src):
+        for way in range(2):
+            n = 2 * flip + way
+            push(24 + n, src.at[pl.ds(2 * way, 2)], midway.at[n], device(ways[way], 0))
+
+    def pass_on(flip):
+        for way in range(2):
+            n = 2 * flip + way
+            arrive(24 + n, midway.at[n])
+            push(28 + n, midway.at[n], spot(-ways[way], flip, 2 * way, 2), device(ways[way], 0))
+
     for step in (4, 3, 5):
         finish(step)
     pl.semaphore_wait(barrier, len(peers))
@@ -625,20 +638,30 @@
             finish(step)
         if step:
             push(step, part(step, 1), relay.at[step - 1], partner)
-            push(8 + step, part(step, 0), spot(0, 0), device(step, 0))
         else:
             push(0, part(0, 1), spot(0, 0), partner)
+        if step == 4:
+            half_way(0, part(4, 0))
+        elif step:
+            push(8 + step, part(step, 0), spot(0, 0), device(step, 0))
+    pass_on(0)
     own = pltpu.make_async_copy(part(0, 0), spot(0, 0), own_sem)
     own.start()
     for step in steps[:-1]:
         arrive(step, relay.at[step - 1])
-        push(16 + step, relay.at[step - 1], spot(0, 1), device(step, 0))
+        if step == 4:
+            half_way(1, relay.at[3])
+        else:
+            push(16 + step, relay.at[step - 1], spot(0, 1), device(step, 0))
+        if step == 2:
+            pass_on(1)
     own.wait()
     arrive(0, spot(0, 1))
-    for step in steps[:-1]:
-        arrive(8 + step, spot(-step, 0))
-    for step in steps[:-1]:
-        arrive(16 + step, spot(-step, 1))
+    for flip in range(2):
+        for step in steps[1:-1]:
+            arrive(8 + flip * 8 + step, spot(-step, flip))
+        for way in range(2):
+            arrive(28 + 2 * flip + way, spot(4, flip, 2 * way, 2))
     for copy in copies:
         copy.wait_send()
 
@@ -650,7 +673,10 @@
         out_shape=jax.ShapeDtypeStruct((64, 64, 128), BF16),
         in_specs=[whole] * 6,
         out_specs=whole,
-        scratch_shapes=[VMEM((2, 8, 4, 64, 128), BF16), VMEM((7, 4, 64, 128), BF16), DMA((24,)), DMA((24,)), DMA],
+        scratch_shapes=[
+            VMEM((2, 8, 4, 64, 128), BF16), VMEM((7, 4, 64, 128), BF16),
+            VMEM((4, 2, 64, 128), BF16), DMA((32,)), DMA((32,)), DMA,
+        ],
         compiler_params=pltpu.CompilerParams(
             collective_id=1, has_side_effects=True, vmem_limit_bytes=16 * 1024 * 1024
         ),

time: 170 us -> 181 us (1.065)
  Pallas kernels: 169 us -> 180 us
    pallas_call x1, Pallas kernels: 92.9 us -> 104 us  [attend(): pl.pallas_call(attend_kernel, out_shape=[jax.ShapeDtypeStruct((18, 64, 25...]
where the time goes in v9:
time: 181 us
  Pallas kernels  180 us (99%)
    pallas_call x1, Pallas kernels, attend(): pl.pallas_call(attend_kernel, out_shape=[jax.ShapeDtypeStruct((18, 64, 25...  104 us
    pallas_call x1, Pallas kernels, spread(): pl.pallas_call(spread_kernel, out_shape=(jax.ShapeDtypeStruct((2, 4, 1024...  47.4 us
    pallas_call x1, Pallas kernels, deliver(): pl.pallas_call(deliver_kernel, out_shape=jax.ShapeDtypeStruct((64, 64, 12...  28.4 us

profile of v9, /device:TPU:1, one launch (start us, length us, event | category | flops | bytes accessed | tf_op | source)
XLA Modules:
  0.0 180.7 jit_solution(5889667065280399182)
XLA Ops:
  0.0 47.4 %spread.1 = (bf16[2,4,1024,128]{3,2,1,0:T(8,128)(2,1)S(1)}, bf16[4,16,128,256]{3,2,1,0:T(8,128)(2,1)S(1)}, bf16[4,16,256,128]{3,2,1,0:T(8,128)(2,1)S(1)}, bf16[2...) custom-call(bf16[128,64,128]{2,1,0:T(8,128)(2,1)} %tile_ref.1, ...), custom_call_target="tpu_custom_call" | custom-call | tf_op jit(solution)/shard_map/spread/pallas_call | solution.py:431
  47.5 103.8 %attend.1 = (f32[18,64,256]{2,1,0:T(8,128)S(1)}, f32[18,64,256]{2,1,0:T(8,128)S(1)}, f32[18,64,256]{2,1,0:T(8,128)S(1)}, f32[18,64,256]{2,1,0:T(8,128)S(1)}) custom-call(s32[8,128]{1,0:T(8,128)S(1)} %get-tuple-element.16.lists_ref, bf16[2,4,1024,128]{3,2,1,0:T(8,128)(2,1)S(1)} %get-tuple-element.17.qg_ref, ...), custom_call_target="tpu_custom_call" | custom-call | tf_op jit(solution)/shard_map/attend/pallas_call | solution.py:555
  151.3 28.4 %deliver.1 = bf16[64,64,128]{2,1,0:T(8,128)(2,1)S(1)} custom-call(f32[18,64,256]{2,1,0:T(8,128)S(1)} %get-tuple-element.22.acc0, f32[18,64,256]{2,1,0:T(8,128)S(1)} %get-tuple-element.23.acc1, f32[18,64,256]{2,1,0:T(8,128)S(1)} %get-tuple-element.24.acc2, f32[18,64,256]{2,1,0:T(8,128)S(1)} %get-tuple-element.25.acc3, ...), custom_call_target="tpu_custom_call" | custom-call | tf_op jit(solution)/shard_map/deliver/pallas_call | solution.py:671
  179.7 1.0 copy.12

commit v10 on v8

--- a/solution.py
+++ b/solution.py
@@ -66,6 +66,17 @@
     for load in loads:
         load.start()
     tops[...] = jnp.zeros_like(tops)
+    for load in loads[1:]:
+        load.wait()
+    wbuf[head, 256:272, :] = jnp.concatenate(
+        [wb_ref[...].astype(F32), jnp.zeros((14, 128), F32)], axis=0
+    ).astype(BF16)
+    pl.semaphore_wait(barrier, len(peers))
+    w_copy = pltpu.make_async_remote_copy(
+        src_ref=wbuf.at[head], dst_ref=wbuf.at[head], send_sem=w_send, recv_sem=w_recv,
+        device_id=partner, device_id_type=MESH,
+    )
+    w_copy.start()
     loads[0].wait()
 
     def widen(block, carry):
@@ -75,7 +86,6 @@
 
     lax.fori_loop(0, 16, widen, 0)
     ones = jnp.ones((128, 128), BF16)
-    loads[1].wait()
     gain = gain_ref[...]
 
     def norm_for(step):
@@ -94,23 +104,7 @@
         norm_for(-n)
         return carry
 
-    def norm_far(n, carry):
-        norm_for(3 + n)
-        norm_for(-3 * (1 - n))
-        return carry
-
     lax.fori_loop(1, 3, norm_near, 0)
-    for load in loads[2:]:
-        load.wait()
-    wbuf[head, 256:272, :] = jnp.concatenate(
-        [wb_ref[...].astype(F32), jnp.zeros((14, 128), F32)], axis=0
-    ).astype(BF16)
-    pl.semaphore_wait(barrier, len(peers))
-    w_copy = pltpu.make_async_remote_copy(
-        src_ref=wbuf.at[head], dst_ref=wbuf.at[head], send_sem=w_send, recv_sem=w_recv,
-        device_id=partner, device_id_type=MESH,
-    )
-    w_copy.start()
     sent = [w_copy]
 
     def push(src, dst, send_sem, recv_sem, device):
@@ -131,7 +125,6 @@
 
     col_push(1)
     col_push(7)
-    lax.fori_loop(0, 2, norm_far, 0)
     pltpu.make_async_remote_copy(
         src_ref=wbuf.at[1 - head], dst_ref=wbuf.at[1 - head], send_sem=w_send, recv_sem=w_recv,
         device_id=partner, device_id_type=MESH,
@@ -141,13 +134,22 @@
     weighted = wb * gain
     wbt = wb.astype(BF16)
 
-    def bias_for(target, carry):
+    def bias_for(step):
+        target = ring(row + step, 8)
         part = lax.dot_general(wbt, send[target].reshape(512, 128), NT, preferred_element_type=F32)
         for jj in range(4):
             flat[pl.ds(pl.multiple_of((4 * target + jj) * 8, 8), 8), :] = part[0:8, jj * 128:jj * 128 + 128]
+
+    def norm_far(n, carry):
+        far = (3 + n, -3 * (1 - n))
+        near = (1 + n, -1 - n)
+        for step in far:
+            norm_for(step)
+        for step in near + far:
+            bias_for(step)
         return carry
 
-    lax.fori_loop(0, 8, bias_for, 0, unroll=4)
+    lax.fori_loop(0, 2, norm_far, 0)
     living = jnp.broadcast_to(types_ref[pl.ds(row, 1), :] != 0, (32, 128))
     by_head = [
         jnp.where(living, flat[pl.ds(h, 32, stride=8), :] * LOG2E, masked_score) for h in range(4)
@@ -252,16 +254,24 @@
         for i in range(16):
             before.append(before[-1] + allowed[i:i + 1, :])
         rank = jnp.concatenate(before[:16], axis=0)
-        pairs = jnp.broadcast_to(jnp.floor((before[16] + 1.0) * 0.5), (16, 128))
+        pairs = jnp.broadcast_to(jnp.floor(before[16] * 0.5), (16, 128))
+        single = jnp.broadcast_to(before[16], (16, 128)) - 2.0 * pairs
+        alone = allowed * jnp.where(rank == 2.0 * pairs, 1.0, 0.0)
+        allowed = allowed - alone
         earlier = (
             lax.broadcasted_iota(jnp.int32, (128, 128), 0) < lax.broadcasted_iota(jnp.int32, (128, 128), 1)
         ).astype(F32).astype(BF16)
         start = jnp.dot(pairs.astype(BF16), earlier, preferred_element_type=F32)
         total = jnp.sum(pairs[0:1, :], axis=1, keepdims=True)
+        single_start = jnp.dot(single.astype(BF16), earlier, preferred_element_type=F32)
+        singles = jnp.sum(single[0:1, :], axis=1, keepdims=True)
         rank = rank + 2.0 * start
         entry = 2.0 * lax.broadcasted_iota(jnp.int32, (16, 128), 1).astype(F32)
         number = lax.broadcasted_iota(jnp.int32, (16, 128), 0).astype(F32)
         block = jnp.zeros((16, 128), F32)
+        single_block = jnp.zeros((16, 128), F32)
+        single_picked = jnp.zeros((16, 128), F32)
+        single_found = jnp.zeros((16, 128), F32)
         picked = [jnp.zeros((16, 128), F32)] * 2
         found = [jnp.zeros((16, 128), F32)] * 2
         for k in range(16):
@@ -273,12 +283,22 @@
                 picked[side] = picked[side] + hit * number
                 if side == 0:
                     block = block + hit * k
+            at = jnp.broadcast_to(single_start[:, k:k + 1], (16, 128))
+            here = jnp.broadcast_to(alone[:, k:k + 1], (16, 128))
+            hit = jnp.where(2.0 * at == entry, here, 0.0)
+            single_found = single_found + hit
+            single_picked = single_picked + hit * number
+            single_block = single_block + hit * k
         rows = [jnp.sum(block, axis=0, keepdims=True)]
         for side in range(2):
             missing = 1.0 - jnp.sum(found[side], axis=0, keepdims=True)
             rows.append(jnp.sum(picked[side], axis=0, keepdims=True) + (16.0 + side) * missing)
         rows.append(jnp.broadcast_to(total, (1, 128)))
-        rows.append(jnp.zeros((4, 128), F32))
+        missing = 1.0 - jnp.sum(single_found, axis=0, keepdims=True)
+        rows.append(jnp.sum(single_block, axis=0, keepdims=True))
+        rows.append(jnp.sum(single_picked, axis=0, keepdims=True) + 16.0 * missing)
+        rows.append(jnp.broadcast_to(singles, (1, 128)))
+        rows.append(jnp.zeros((1, 128), F32))
         lists_ref[...] = jnp.concatenate(rows, axis=0).astype(jnp.int32)
 
     own_cols.wait()
@@ -517,16 +537,31 @@
                         accs[j][ids[n]] = olds[n] + total[n * 64:(n + 1) * 64, :]
             return carry
 
+        def single_step(t, carry):
+            for j in range(4):
+                for side in range(4):
+                    e = 4 * t + side
+                    block = lists_ref[4, e]
+                    i = lists_ref[5, e]
+                    offset = jnp.concatenate(offset_of(i, block), axis=0)
+                    score = jnp.dot(query(j, i), kbd[j, block], preferred_element_type=F32)
+                    weights = jnp.exp2(score + offset).astype(BF16)
+                    total = jnp.dot(weights, values_of(j, block), preferred_element_type=F32)
+                    accs[j][i] = accs[j][i] + total
+            return carry
+
         lax.fori_loop(0, lax.div(total_pairs + 1, 2), step, 0)
+        lax.fori_loop(0, lax.div(lists_ref[6, 0] + 3, 4), single_step, 0)
 
     @pl.when(jnp.logical_not(safe))
     def _():
         peak[...] = jnp.full_like(peak, -1e30)
 
         def step(n, carry):
-            e = lax.div(n, 2)
-            block = lists_ref[0, e]
-            i = lists_ref[1 + lax.rem(n, 2), e]
+            e = jnp.where(n < 2 * total_pairs, lax.div(n, 2), n - 2 * total_pairs)
+            line = jnp.where(n < 2 * total_pairs, lax.rem(n, 2), 4)
+            block = lists_ref[jnp.where(line == 4, 4, 0), e]
+            i = lists_ref[1 + line, e]
             offset = jnp.concatenate(offset_of(i, block), axis=0)
             for j in range(4):
                 score = jnp.dot(query(j, i), kbd[j, block], preferred_element_type=F32) + offset
@@ -547,7 +582,7 @@
                 peak[j, i] = fresh
             return carry
 
-        lax.fori_loop(0, 2 * total_pairs, step, 0)
+        lax.fori_loop(0, 2 * total_pairs + lists_ref[6, 0], step, 0)
 
 
 def attend(lists, qg, kbd, vbd, bias, bound):

time: 170 us -> 167 us (0.982)
  Pallas kernels: 169 us -> 166 us
    pallas_call x1, Pallas kernels: 92.9 us -> 89.2 us  [attend(): pl.pallas_call(attend_kernel, out_shape=[jax.ShapeDtypeStruct((18, 64, 25...]
where the time goes in v10:
time: 167 us
  Pallas kernels  166 us (99%)
    pallas_call x1, Pallas kernels, attend(): pl.pallas_call(attend_kernel, out_shape=[jax.ShapeDtypeStruct((18, 64, 25...  89.2 us
    pallas_call x1, Pallas kernels, spread(): pl.pallas_call(spread_kernel, out_shape=(jax.ShapeDtypeStruct((2, 4, 1024...  47.8 us
    pallas_call x1, Pallas kernels, deliver(): pl.pallas_call(deliver_kernel, out_shape=jax.ShapeDtypeStruct((64, 64, 12...  28.7 us

profile of v10, /device:TPU:1, one launch (start us, length us, event | category | flops | bytes accessed | tf_op | source)
XLA Modules:
  0.0 166.7 jit_solution(3807512344332229882)
XLA Ops:
  0.0 47.8 %spread.1 = (bf16[2,4,1024,128]{3,2,1,0:T(8,128)(2,1)S(1)}, bf16[4,16,128,256]{3,2,1,0:T(8,128)(2,1)S(1)}, bf16[4,16,256,128]{3,2,1,0:T(8,128)(2,1)S(1)}, bf16[2...) custom-call(bf16[128,64,128]{2,1,0:T(8,128)(2,1)} %tile_ref.1, ...), custom_call_target="tpu_custom_call" | custom-call | tf_op jit(solution)/shard_map/spread/pallas_call | solution.py:451
  47.8 89.2 %attend.1 = (f32[18,64,256]{2,1,0:T(8,128)S(1)}, f32[18,64,256]{2,1,0:T(8,128)S(1)}, f32[18,64,256]{2,1,0:T(8,128)S(1)}, f32[18,64,256]{2,1,0:T(8,128)S(1)}) custom-call(s32[8,128]{1,0:T(8,128)S(1)} %get-tuple-element.16.lists_ref, bf16[2,4,1024,128]{3,2,1,0:T(8,128)(2,1)S(1)} %get-tuple-element.17.qg_ref, ...), custom_call_target="tpu_custom_call" | custom-call | tf_op jit(solution)/shard_map/attend/pallas_call | solution.py:590
  137.0 28.7 %deliver.1 = bf16[64,64,128]{2,1,0:T(8,128)(2,1)S(1)} custom-call(f32[18,64,256]{2,1,0:T(8,128)S(1)} %get-tuple-element.22.acc0, f32[18,64,256]{2,1,0:T(8,128)S(1)} %get-tuple-element.23.acc1, f32[18,64,256]{2,1,0:T(8,128)S(1)} %get-tuple-element.24.acc2, f32[18,64,256]{2,1,0:T(8,128)S(1)} %get-tuple-element.25.acc3, ...), custom_call_target="tpu_custom_call" | custom-call | tf_op jit(solution)/shard_map/deliver/pallas_call | solution.py:683
  165.7 1.0 copy.12

commit v11 on v10

--- a/solution.py
+++ b/solution.py
@@ -66,7 +66,41 @@
     for load in loads:
         load.start()
     tops[...] = jnp.zeros_like(tops)
-    for load in loads[1:]:
+    loads[0].wait()
+
+    def widen(block, carry):
+        rows = half[pl.ds(block * 8, 8)].astype(F32).reshape(256, 128)
+        wide[pl.ds(pl.multiple_of(block * 256, 256), 256), :] = rows
+        return carry
+
+    lax.fori_loop(0, 16, widen, 0)
+    ones = jnp.ones((128, 128), BF16)
+    loads[1].wait()
+    gain = gain_ref[...]
+
+    def norm_for(step):
+        target = ring(row + step, 8)
+        for jj in range(4):
+            value = wide[pl.ds(4 * target + jj, 128, stride=32), :]
+            mean = jnp.dot(value.astype(BF16), ones, preferred_element_type=F32) * (1.0 / 128)
+            centred = value - mean
+            squares = (centred * centred).astype(BF16)
+            spread = jnp.dot(squares, ones, preferred_element_type=F32) * (1.0 / 128)
+            normed = centred * lax.rsqrt(spread + epsilon) * gain
+            send[target, jj] = normed.astype(BF16)
+
+    def norm_near(n, carry):
+        norm_for(n)
+        norm_for(-n)
+        return carry
+
+    def norm_far(n, carry):
+        norm_for(3 + n)
+        norm_for(-3 * (1 - n))
+        return carry
+
+    lax.fori_loop(1, 3, norm_near, 0)
+    for load in loads[2:]:
         load.wait()
     wbuf[head, 256:272, :] = jnp.concatenate(
         [wb_ref[...].astype(F32), jnp.zeros((14, 128), F32)], axis=0
@@ -77,34 +111,6 @@
         device_id=partner, device_id_type=MESH,
     )
     w_copy.start()
-    loads[0].wait()
-
-    def widen(block, carry):
-        rows = half[pl.ds(block * 8, 8)].astype(F32).reshape(256, 128)
-        wide[pl.ds(pl.multiple_of(block * 256, 256), 256), :] = rows
-        return carry
-
-    lax.fori_loop(0, 16, widen, 0)
-    ones = jnp.ones((128, 128), BF16)
-    gain = gain_ref[...]
-
-    def norm_for(step):
-        target = ring(row + step, 8)
-        for jj in range(4):
-            value = wide[pl.ds(4 * target + jj, 128, stride=32), :]
-            mean = jnp.dot(value.astype(BF16), ones, preferred_element_type=F32) * (1.0 / 128)
-            centred = value - mean
-            squares = (centred * centred).astype(BF16)
-            spread = jnp.dot(squares, ones, preferred_element_type=F32) * (1.0 / 128)
-            normed = centred * lax.rsqrt(spread + epsilon) * gain
-            send[target, jj] = normed.astype(BF16)
-
-    def norm_near(n, carry):
-        norm_for(n)
-        norm_for(-n)
-        return carry
-
-    lax.fori_loop(1, 3, norm_near, 0)
     sent = [w_copy]
 
     def push(src, dst, send_sem, recv_sem, device):
@@ -125,6 +131,7 @@
 
     col_push(1)
     col_push(7)
+    lax.fori_loop(0, 2, norm_far, 0)
     pltpu.make_async_remote_copy(
         src_ref=wbuf.at[1 - head], dst_ref=wbuf.at[1 - head], send_sem=w_send, recv_sem=w_recv,
         device_id=partner, device_id_type=MESH,
@@ -134,22 +141,13 @@
     weighted = wb * gain
     wbt = wb.astype(BF16)
 
-    def bias_for(step):
-        target = ring(row + step, 8)
+    def bias_for(target, carry):
         part = lax.dot_general(wbt, send[target].reshape(512, 128), NT, preferred_element_type=F32)
         for jj in range(4):
             flat[pl.ds(pl.multiple_of((4 * target + jj) * 8, 8), 8), :] = part[0:8, jj * 128:jj * 128 + 128]
-
-    def norm_far(n, carry):
-        far = (3 + n, -3 * (1 - n))
-        near = (1 + n, -1 - n)
-        for step in far:
-            norm_for(step)
-        for step in near + far:
-            bias_for(step)
         return carry
 
-    lax.fori_loop(0, 2, norm_far, 0)
+    lax.fori_loop(0, 8, bias_for, 0, unroll=4)
     living = jnp.broadcast_to(types_ref[pl.ds(row, 1), :] != 0, (32, 128))
     by_head = [
         jnp.where(living, flat[pl.ds(h, 32, stride=8), :] * LOG2E, masked_score) for h in range(4)
@@ -518,10 +516,10 @@
 
     @pl.when(safe)
     def _():
-        def step(t, carry):
+        def pairs_from(first, count):
             work = []
-            for side in range(2):
-                e = 2 * t + side
+            for side in range(count):
+                e = first + side
                 block = lists_ref[0, e]
                 ids = (lists_ref[1, e], lists_ref[2, e])
                 offset = jnp.concatenate(offset_of(ids[0], block) + offset_of(ids[1], block), axis=0)
@@ -535,6 +533,13 @@
                     olds = [accs[j][i] for i in ids]
                     for n in range(2):
                         accs[j][ids[n]] = olds[n] + total[n * 64:(n + 1) * 64, :]
+
+        def four_step(t, carry):
+            pairs_from(4 * t, 4)
+            return carry
+
+        def two_step(t, carry):
+            pairs_from(2 * t, 2)
             return carry
 
         def single_step(t, carry):
@@ -550,7 +555,9 @@
                     accs[j][i] = accs[j][i] + total
             return carry
 
-        lax.fori_loop(0, lax.div(total_pairs + 1, 2), step, 0)
+        fours = lax.div(total_pairs, 4)
+        lax.fori_loop(0, fours, four_step, 0)
+        lax.fori_loop(2 * fours, lax.div(total_pairs + 1, 2), two_step, 0)
         lax.fori_loop(0, lax.div(lists_ref[6, 0] + 3, 4), single_step, 0)
 
     @pl.when(jnp.logical_not(safe))

time: 167 us -> 170 us (1.018)
  Pallas kernels: 166 us -> 169 us
    pallas_call x1, Pallas kernels: 89.2 us -> 92.9 us  [attend(): pl.pallas_call(attend_kernel, out_shape=[jax.ShapeDtypeStruct((18, 64, 25...]
where the time goes in v11:
time: 170 us
  Pallas kernels  169 us (99%)
    pallas_call x1, Pallas kernels, attend(): pl.pallas_call(attend_kernel, out_shape=[jax.ShapeDtypeStruct((18, 64, 25...  92.9 us
    pallas_call x1, Pallas kernels, spread(): pl.pallas_call(spread_kernel, out_shape=(jax.ShapeDtypeStruct((2, 4, 1024...  47.4 us
    pallas_call x1, Pallas kernels, deliver(): pl.pallas_call(deliver_kernel, out_shape=jax.ShapeDtypeStruct((64, 64, 12...  28.3 us

profile of v11, /device:TPU:1, one launch (start us, length us, event | category | flops | bytes accessed | tf_op | source)
XLA Modules:
  0.0 169.6 jit_solution(6182692103552105218)
XLA Ops:
  0.0 47.4 %spread.1 = (bf16[2,4,1024,128]{3,2,1,0:T(8,128)(2,1)S(1)}, bf16[4,16,128,256]{3,2,1,0:T(8,128)(2,1)S(1)}, bf16[4,16,256,128]{3,2,1,0:T(8,128)(2,1)S(1)}, bf16[2...) custom-call(bf16[128,64,128]{2,1,0:T(8,128)(2,1)} %tile_ref.1, ...), custom_call_target="tpu_custom_call" | custom-call | tf_op jit(solution)/shard_map/spread/pallas_call | solution.py:449
  47.5 92.9 %attend.1 = (f32[18,64,256]{2,1,0:T(8,128)S(1)}, f32[18,64,256]{2,1,0:T(8,128)S(1)}, f32[18,64,256]{2,1,0:T(8,128)S(1)}, f32[18,64,256]{2,1,0:T(8,128)S(1)}) custom-call(s32[8,128]{1,0:T(8,128)S(1)} %get-tuple-element.16.lists_ref, bf16[2,4,1024,128]{3,2,1,0:T(8,128)(2,1)S(1)} %get-tuple-element.17.qg_ref, ...), custom_call_target="tpu_custom_call" | custom-call | tf_op jit(solution)/shard_map/attend/pallas_call | solution.py:597
  140.3 28.3 %deliver.1 = bf16[64,64,128]{2,1,0:T(8,128)(2,1)S(1)} custom-call(f32[18,64,256]{2,1,0:T(8,128)S(1)} %get-tuple-element.22.acc0, f32[18,64,256]{2,1,0:T(8,128)S(1)} %get-tuple-element.23.acc1, f32[18,64,256]{2,1,0:T(8,128)S(1)} %get-tuple-element.24.acc2, f32[18,64,256]{2,1,0:T(8,128)S(1)} %get-tuple-element.25.acc3, ...), custom_call_target="tpu_custom_call" | custom-call | tf_op jit(solution)/shard_map/deliver/pallas_call | solution.py:690
  168.6 1.0 copy.12

commit v12 on v11

--- a/solution.py
+++ b/solution.py
@@ -385,7 +385,7 @@
         begin(0, run)
     for run in range(2):
         across(0, run, 0)
-    for step in (2, 6, 3, 5, 4):
+    for step in (4, 3, 5, 2, 6):
         col_push(step)
     take(1)
     take(-1)
@@ -411,7 +411,7 @@
             across(far, run, 3)
     for run in range(2):
         to_sibling(run, 3, 0)
-    take(2)
+    take(4)
     for u in range(4):
         for far in range(2):
             for run in range(2):
@@ -420,17 +420,17 @@
             to_sibling(run, u, 1)
             to_sibling(run, u, 2)
         if u == 1:
-            take(-2)
+            take(3)
         if u == 3:
-            take(3)
+            take(-3)
     for u in range(4):
         for run in range(2):
             for far in range(2):
                 end_second(far, run, u)
             to_sibling(run, u, 3)
         if u == 2:
-            take(-3)
-    take(4)
+            take(2)
+    take(-2)
     bound_ref[0:8, :] = tops[...]
     bound_ref[8:24, :] = jnp.broadcast_to(jnp.sum(weighted * weighted, axis=1, keepdims=True), (16, 128))
     for run in range(2):

time: 170 us -> 159 us (0.935)
  Pallas kernels: 169 us -> 157 us
    pallas_call x1, Pallas kernels: 92.9 us -> 80 us  [attend(): pl.pallas_call(attend_kernel, out_shape=[jax.ShapeDtypeStruct((18, 64, 25...]
where the time goes in v12:
time: 159 us; the launch traced here: 158 us
  Pallas kernels  157 us (99%)
    pallas_call x1, Pallas kernels, attend(): pl.pallas_call(attend_kernel, out_shape=[jax.ShapeDtypeStruct((18, 64, 25...  80 us
    pallas_call x1, Pallas kernels, spread(): pl.pallas_call(spread_kernel, out_shape=(jax.ShapeDtypeStruct((2, 4, 1024...  49 us
    pallas_call x1, Pallas kernels, deliver(): pl.pallas_call(deliver_kernel, out_shape=jax.ShapeDtypeStruct((64, 64, 12...  28.4 us

profile of v12, /device:TPU:1, one launch (start us, length us, event | category | flops | bytes accessed | tf_op | source)
XLA Modules:
  0.0 158.5 jit_solution(12103936535553318004)
XLA Ops:
  0.0 49.0 %spread.1 = (bf16[2,4,1024,128]{3,2,1,0:T(8,128)(2,1)S(1)}, bf16[4,16,128,256]{3,2,1,0:T(8,128)(2,1)S(1)}, bf16[4,16,256,128]{3,2,1,0:T(8,128)(2,1)S(1)}, bf16[2...) custom-call(bf16[128,64,128]{2,1,0:T(8,128)(2,1)} %tile_ref.1, ...), custom_call_target="tpu_custom_call" | custom-call | tf_op jit(solution)/shard_map/spread/pallas_call | solution.py:449
  49.0 80.0 %attend.1 = (f32[18,64,256]{2,1,0:T(8,128)S(1)}, f32[18,64,256]{2,1,0:T(8,128)S(1)}, f32[18,64,256]{2,1,0:T(8,128)S(1)}, f32[18,64,256]{2,1,0:T(8,128)S(1)}) custom-call(s32[8,128]{1,0:T(8,128)S(1)} %get-tuple-element.16.lists_ref, bf16[2,4,1024,128]{3,2,1,0:T(8,128)(2,1)S(1)} %get-tuple-element.17.qg_ref, ...), custom_call_target="tpu_custom_call" | custom-call | tf_op jit(solution)/shard_map/attend/pallas_call | solution.py:597
  129.1 28.4 %deliver.1 = bf16[64,64,128]{2,1,0:T(8,128)(2,1)S(1)} custom-call(f32[18,64,256]{2,1,0:T(8,128)S(1)} %get-tuple-element.22.acc0, f32[18,64,256]{2,1,0:T(8,128)S(1)} %get-tuple-element.23.acc1, f32[18,64,256]{2,1,0:T(8,128)S(1)} %get-tuple-element.24.acc2, f32[18,64,256]{2,1,0:T(8,128)S(1)} %get-tuple-element.25.acc3, ...), custom_call_target="tpu_custom_call" | custom-call | tf_op jit(solution)/shard_map/deliver/pallas_call | solution.py:690
  157.5 1.0 copy.12

commit v13 on v11

--- a/solution.py
+++ b/solution.py
@@ -619,7 +619,7 @@
     def device(step, flip):
         return (ring(row + step, 8), col, other(flip))
 
-    steps = (4, 3, 5, 2, 6, 1, 7, 0)
+    steps = (1, 7, 2, 6, 3, 5, 4, 0)
     partner = device(0, 1)
     peers = [partner] + [device(step, 0) for step in steps if step]
     barrier = pltpu.get_barrier_semaphore()
@@ -659,11 +659,11 @@
             device_id=partner, device_id_type=MESH,
         ).wait_recv()
 
-    for step in (4, 3, 5):
+    for step in (1, 7, 2):
         finish(step)
     pl.semaphore_wait(barrier, len(peers))
     for step in steps:
-        if step not in (4, 3, 5):
+        if step not in (1, 7, 2):
             finish(step)
         if step:
             push(step, part(step, 1), relay.at[step - 1], partner)

time: 170 us -> 156 us (0.918)
  Pallas kernels: 169 us -> 155 us
    pallas_call x1, Pallas kernels: 92.9 us -> 80 us  [attend(): pl.pallas_call(attend_kernel, out_shape=[jax.ShapeDtypeStruct((18, 64, 25...]
where the time goes in v13:
time: 156 us
  Pallas kernels  155 us (99%)
    pallas_call x1, Pallas kernels, attend(): pl.pallas_call(attend_kernel, out_shape=[jax.ShapeDtypeStruct((18, 64, 25...  80 us
    pallas_call x1, Pallas kernels, spread(): pl.pallas_call(spread_kernel, out_shape=(jax.ShapeDtypeStruct((2, 4, 1024...  47.4 us
    pallas_call x1, Pallas kernels, deliver(): pl.pallas_call(deliver_kernel, out_shape=jax.ShapeDtypeStruct((64, 64, 12...  27.3 us

profile of v13, /device:TPU:1, one launch (start us, length us, event | category | flops | bytes accessed | tf_op | source)
XLA Modules:
  0.0 155.8 jit_solution(8580528795378323072)
XLA Ops:
  0.0 47.4 %spread.1 = (bf16[2,4,1024,128]{3,2,1,0:T(8,128)(2,1)S(1)}, bf16[4,16,128,256]{3,2,1,0:T(8,128)(2,1)S(1)}, bf16[4,16,256,128]{3,2,1,0:T(8,128)(2,1)S(1)}, bf16[2...) custom-call(bf16[128,64,128]{2,1,0:T(8,128)(2,1)} %tile_ref.1, ...), custom_call_target="tpu_custom_call" | custom-call | tf_op jit(solution)/shard_map/spread/pallas_call | solution.py:449
  47.5 80.0 %attend.1 = (f32[18,64,256]{2,1,0:T(8,128)S(1)}, f32[18,64,256]{2,1,0:T(8,128)S(1)}, f32[18,64,256]{2,1,0:T(8,128)S(1)}, f32[18,64,256]{2,1,0:T(8,128)S(1)}) custom-call(s32[8,128]{1,0:T(8,128)S(1)} %get-tuple-element.16.lists_ref, bf16[2,4,1024,128]{3,2,1,0:T(8,128)(2,1)S(1)} %get-tuple-element.17.qg_ref, ...), custom_call_target="tpu_custom_call" | custom-call | tf_op jit(solution)/shard_map/attend/pallas_call | solution.py:597
  127.5 27.3 %deliver.1 = bf16[64,64,128]{2,1,0:T(8,128)(2,1)S(1)} custom-call(f32[18,64,256]{2,1,0:T(8,128)S(1)} %get-tuple-element.22.acc0, f32[18,64,256]{2,1,0:T(8,128)S(1)} %get-tuple-element.23.acc1, f32[18,64,256]{2,1,0:T(8,128)S(1)} %get-tuple-element.24.acc2, f32[18,64,256]{2,1,0:T(8,128)S(1)} %get-tuple-element.25.acc3, ...), custom_call_target="tpu_custom_call" | custom-call | tf_op jit(solution)/shard_map/deliver/pallas_call | solution.py:690
  154.8 1.0 copy.12
